TPU v7x, 32 devices: a whole 2x2x4 slice. The times are simulated.
32 devices in a mesh: row: 8 (over y, x, core), col: 4 (over z).
Axes of the slice: x: 2, y: 2, z: 4, core: 2. Of those that a mesh axis runs over, the one named last changes fastest.
Arguments:
- kernel: bfloat16 [16, 8, 16, 4, 8192], P(None, 'row', None, 'col'), as said below
Outputs:
- factor: float32 [16, 8, 16, 4, 8192], P(None, 'row', None, 'col')
Inputs may be any that keep to these rules, and one draw needn't show every extreme that they name: kernel holds a symmetric positive definite matrix.
All inputs are finite; a program needn't handle non-finite values.
Results may differ from a plain program's by a relative error of at most 0.0046.
Values may be sent and summed in bfloat16 or wider, within the bound.
No kernel may reach another device: no remote copies, remote signals or barrier semaphores. Data moves between devices by JAX's collectives and lax.ppermute only.
A program may use at most 64 MiB of HBM per device.

v0:
```python
import functools

import jax
import jax.numpy as jnp
from jax import lax
from jax.experimental import pallas as pl
from jax.experimental.pallas import tpu as pltpu
from jax.sharding import PartitionSpec as P

P_SIZE = 512
NT = 16
STEP = 16
BLOCK = 128
EXACT = lax.Precision.HIGHEST


def exact_dot(left_side, right_side, contract=((1,), (0,))):
    return lax.dot_general(
        left_side,
        right_side,
        (contract, ((), ())),
        preferred_element_type=jnp.float32,
        precision=EXACT,
    )


def split(value):
    high = value.astype(jnp.bfloat16)
    return high, (value - high.astype(jnp.float32)).astype(jnp.bfloat16)


def split_three(value):
    high = value.astype(jnp.bfloat16)
    value = value - high.astype(jnp.float32)
    return high, *split(value)


def beside(parts):
    return jnp.concatenate(parts, axis=1)


def fast_dot(left_side, right_side, contract=((1,), (0,))):
    return lax.dot_general(
        left_side, right_side, (contract, ((), ())), preferred_element_type=jnp.float32
    )


def repeat_columns(rows, start):
    slots = BLOCK // STEP
    slot = lax.broadcasted_iota(jnp.int32, rows.shape, 1) // STEP
    slot = (slot + (slots - start // STEP)) % slots
    spread_out = rows
    for place in range(1, 6):
        spread_out = jnp.where(slot == place, pltpu.roll(rows, place * STEP, 1), spread_out)
    high, middle, low = (part.astype(jnp.float32) for part in split_three(spread_out))
    parts = jnp.where(slot < 3, high, jnp.where(slot < 5, middle, low))
    return jnp.where(slot < 6, parts, 0.0).astype(jnp.bfloat16)


def factor_block(work, done):
    row_id = lax.broadcasted_iota(jnp.int32, (STEP, BLOCK), 0)
    for start in range(0, BLOCK, STEP):
        here = slice(start, start + STEP)
        halves = [work[here, 0:BLOCK], work[here, BLOCK : 2 * BLOCK]]
        columns = [
            jnp.broadcast_to(halves[0][:, start + j : start + j + 1], (STEP, BLOCK))
            for j in range(STEP)
        ]
        if start + STEP < BLOCK:
            raw = repeat_columns(work[start + STEP :, 0:BLOCK], start)
        kept = [jnp.zeros((STEP, BLOCK), jnp.float32)] * 2
        pivots = jnp.ones((STEP, BLOCK), jnp.float32)
        for k in range(STEP):
            pivot = jnp.broadcast_to(columns[k][k : k + 1, :], (STEP, BLOCK))
            factors = jnp.where(row_id == k, 0.0, columns[k] * (1.0 / pivot))
            for j in range(k + 1, STEP):
                top = jnp.broadcast_to(columns[j][k : k + 1, :], (STEP, BLOCK))
                columns[j] = columns[j] - factors * top
            pivots = jnp.where(row_id == k, pivot, pivots)
            for h in range(2):
                top = jnp.broadcast_to(halves[h][k : k + 1, :], (STEP, BLOCK))
                kept[h] = jnp.where(row_id == k, top, kept[h])
                halves[h] = halves[h] - factors * top
        scale = lax.rsqrt(pivots)
        inverse = 1.0 / pivots
        for h in range(2):
            done[here, h * BLOCK : (h + 1) * BLOCK] = kept[h] * scale
        if start + STEP < BLOCK:
            solved = jnp.concatenate([halves[0] * inverse, halves[1] * inverse], axis=1)
            high, middle, low = split_three(solved)
            blank = jnp.zeros_like(high)
            parts = [high, middle, low, high, middle, high, blank, blank]
            slots = BLOCK // STEP
            parts = [parts[(at - start // STEP) % slots] for at in range(slots)]
            parts = jnp.concatenate(parts)
            after, later = start + STEP, start + 2 * STEP
            blocks = [(after, later, 0), (later, BLOCK, 0), (after, BLOCK, BLOCK)]
            for first, last, column in blocks:
                if first < last:
                    here = (slice(first, last), slice(column, column + BLOCK))
                    work[here] = work[here] - fast_dot(
                        raw[first - after : last - after], parts[:, column : column + BLOCK]
                    )


def factor_kernel(given, factor, inverse, rest, work, done):
    rest[...] = given[...]
    factor_rest(rest, factor, inverse, work, done)


def factor_rest(rest, factor, inverse, work, done):
    order = rest.shape[0]
    inverse[...] = jnp.zeros_like(inverse)
    factor[...] = jnp.zeros_like(factor)
    row_id = lax.broadcasted_iota(jnp.int32, (BLOCK, BLOCK), 0)
    column_id = lax.broadcasted_iota(jnp.int32, (BLOCK, BLOCK), 1)

    def step(at, carry):
        now = pl.ds(pl.multiple_of(at * BLOCK, BLOCK), BLOCK)
        work[:, 0:BLOCK] = rest[now, now]
        work[:, BLOCK:] = (row_id == column_id).astype(jnp.float32)
        factor_block(work, done)
        factor[now, now] = jnp.where(column_id >= row_id, done[:, 0:BLOCK], 0.0).T
        for start in range(0, order, BLOCK):
            pl.when(at * BLOCK == start)(functools.partial(spread_block, start))
        return carry

    def spread_block(start):
        here = slice(start, start + BLOCK)
        block_inverse = done[:, BLOCK:]
        if start:
            inverse[here, 0:start] = exact_dot(block_inverse, inverse[here, 0:start])
        inverse[here, here] = block_inverse
        if start + BLOCK < order:
            after = slice(start + BLOCK, order)
            upper = exact_dot(block_inverse, rest[here, after])
            lower = upper.T
            factor[after, here] = lower
            rest[after, after] = rest[after, after] - exact_dot(lower, upper)
            so_far = slice(0, start + BLOCK)
            inverse[after, so_far] = inverse[after, so_far] - exact_dot(
                lower, inverse[here, so_far]
            )

    lax.fori_loop(0, order // BLOCK, step, 0)


def factor_scratch():
    return [
        pltpu.VMEM((P_SIZE, P_SIZE), jnp.float32),
        pltpu.VMEM((BLOCK, 2 * BLOCK), jnp.float32),
        pltpu.VMEM((BLOCK, 2 * BLOCK), jnp.float32),
    ]


def factor_corner(corner):
    order = corner.shape[0]
    square = jax.ShapeDtypeStruct((order, order), jnp.float32)
    return pl.pallas_call(
        factor_kernel,
        out_shape=[square, square],
        scratch_shapes=factor_scratch(),
        compiler_params=pltpu.CompilerParams(vmem_limit_bytes=20 * 2**20),
    )(corner)


def spread(value, axis, offsets):
    count = lax.axis_size(axis)
    parts = [value]
    for offset in offsets[1:]:
        parts.append(lax.ppermute(value, axis, [(i, i ^ offset) for i in range(count)]))
    return jnp.stack(parts)


def gather_corner(mine):
    row_count = lax.axis_size("row")
    col_count = lax.axis_size("col")
    row_index = lax.axis_index("row")
    column_index = lax.axis_index("col")
    over_cols = spread(mine, "col", list(range(col_count)))
    over_chips = spread(over_cols, "row", list(range(0, row_count, 2)))
    slots = spread(over_chips, "row", [0, 1])
    slots = slots.transpose(1, 0, 2, 3, 4, 5).reshape(row_count, col_count, *mine.shape)
    slots = jnp.take(slots, jnp.arange(row_count) ^ row_index, axis=0, mode="clip")
    slots = jnp.take(slots, jnp.arange(col_count) ^ column_index, axis=1, mode="clip")
    return slots.transpose(2, 0, 3, 1, 4).reshape(3, P_SIZE, P_SIZE)


def per_device_general(kernel):
    row_count = lax.axis_size("row")
    col_count = lax.axis_size("col")
    tile_rows = P_SIZE // row_count
    tile_cols = P_SIZE // col_count
    row_index = lax.axis_index("row")
    column_index = lax.axis_index("col")
    tiles = kernel.reshape(NT, NT, tile_rows, tile_cols)
    corner = gather_corner(jnp.stack([tiles[0, 0], tiles[1, 0], tiles[1, 1]]))
    own_rows = tiles[:, 0:2].transpose(0, 2, 1, 3).reshape(NT * tile_rows, 2 * tile_cols)
    own_rows = lax.all_gather(own_rows, "col", axis=0, tiled=False)
    own_rows = own_rows.reshape(col_count, NT * tile_rows, 2, tile_cols).transpose(1, 2, 0, 3)
    own_rows = own_rows.reshape(NT * tile_rows, 2, P_SIZE)
    own_cols = tiles[0:2].transpose(0, 2, 1, 3).reshape(2 * tile_rows, NT * tile_cols)
    own_cols = lax.all_gather(own_cols, "row", axis=0, tiled=False)
    own_cols = own_cols.reshape(row_count, 2, tile_rows, NT * tile_cols).transpose(1, 0, 2, 3)
    own_cols = own_cols.reshape(2, P_SIZE, NT * tile_cols)

    first_corner, cross_corner, second_corner = (corner[i].astype(jnp.float32) for i in range(3))
    first_factor, first_inverse = factor_corner(0.5 * (first_corner + first_corner.T))
    cross = exact_dot(cross_corner, first_inverse, ((1,), (1,))).astype(jnp.bfloat16)
    updated_corner = second_corner - fast_dot(cross, cross, ((1,), (1,)))
    second_factor, second_inverse = factor_corner(0.5 * (updated_corner + updated_corner.T))

    first_rows = exact_dot(
        own_rows[tile_rows:, 0].astype(jnp.float32), first_inverse, ((1,), (1,))
    )
    first_cols = exact_dot(first_inverse, own_cols[0, :, tile_cols:].astype(jnp.float32))
    first_rows_rounded = first_rows.astype(jnp.bfloat16)
    first_cols_rounded = first_cols.astype(jnp.bfloat16)
    second_rows = own_rows[2 * tile_rows :, 1].astype(jnp.float32) - fast_dot(
        first_rows_rounded[tile_rows:], cross, ((1,), (1,))
    )
    second_cols = own_cols[1, :, 2 * tile_cols :].astype(jnp.float32) - fast_dot(
        cross, first_cols_rounded[:, tile_cols:]
    )
    second_rows = exact_dot(second_rows, second_inverse, ((1,), (1,)))
    second_cols = exact_dot(second_inverse, second_cols)
    left_side = jnp.concatenate(
        [first_rows_rounded[tile_rows:], second_rows.astype(jnp.bfloat16)], axis=1
    )
    right_side = jnp.concatenate(
        [first_cols_rounded[:, tile_cols:], second_cols.astype(jnp.bfloat16)], axis=0
    )
    inner = NT - 2
    product = fast_dot(left_side, right_side).reshape(inner, tile_rows, inner, tile_cols)
    trailing = tiles[2:, 2:].astype(jnp.float32) - product.transpose(0, 2, 1, 3)
    own = (row_index * tile_rows, column_index * tile_cols)
    first_own = lax.dynamic_slice_in_dim(first_rows, own[1], tile_cols, 1)
    second_own = lax.dynamic_slice_in_dim(second_rows, own[1], tile_cols, 1)
    first_tile = lax.dynamic_slice(first_factor, own, (tile_rows, tile_cols))
    second_tile = lax.dynamic_slice(second_factor, own, (tile_rows, tile_cols))
    result = jnp.zeros(tiles.shape, jnp.float32)
    result = result.at[2:, 2:].set(trailing)
    result = result.at[0, 0].set(first_tile)
    result = result.at[1:, 0].set(first_own.reshape(NT - 1, tile_rows, tile_cols))
    result = result.at[1, 1].set(second_tile)
    result = result.at[2:, 1].set(second_own.reshape(NT - 2, tile_rows, tile_cols))
    return result.reshape(kernel.shape)


def whole(shape):
    return pl.BlockSpec(shape, lambda *_: (0,) * len(shape))


def natural_tile(tiles, spread_rows, tile_rows):
    for r in range(tile_rows):
        spread_rows[r * NT : (r + 1) * NT, :] = tiles[:, r * BLOCK : (r + 1) * BLOCK].astype(
            jnp.float32
        )


def top_kernel(tiles, corner, top, spread_rows):
    tile_rows = corner.shape[1]
    for t in range(2):
        natural_tile(tiles[t], spread_rows, tile_rows)
        for s in range(NT):
            tile = spread_rows[pl.ds(s, tile_rows, stride=NT), :].astype(jnp.bfloat16)
            if s >= 2:
                here = slice((s - 2) * BLOCK, (s - 1) * BLOCK)
                top[t * tile_rows : (t + 1) * tile_rows, here] = tile
            elif s <= t:
                corner[t + s] = tile


def left_kernel(tiles, left, spread_rows):
    tile_rows = left.shape[0] // (NT - 2)
    half = NT // 2
    for t in range(2, NT):
        for r in range(tile_rows):
            part = tiles[t, :, r * BLOCK : (r + 1) * BLOCK].astype(jnp.float32)
            spread_rows[r * half : (r + 1) * half, :] = part[0:half]
        rows = slice((t - 2) * tile_rows, (t - 1) * tile_rows)
        for s in range(2):
            tile = spread_rows[pl.ds(s, tile_rows, stride=half), :].astype(jnp.bfloat16)
            left[rows, s * BLOCK : (s + 1) * BLOCK] = tile


def take_top(tiles, tile_rows):
    return pl.pallas_call(
        top_kernel,
        in_specs=[pl.BlockSpec(memory_space=pltpu.VMEM)],
        out_shape=[
            jax.ShapeDtypeStruct((3, tile_rows, BLOCK), jnp.bfloat16),
            jax.ShapeDtypeStruct((2 * tile_rows, (NT - 2) * BLOCK), jnp.bfloat16),
        ],
        scratch_shapes=[pltpu.VMEM((tile_rows * NT, BLOCK), jnp.float32)],
        compiler_params=pltpu.CompilerParams(vmem_limit_bytes=16 * 2**20),
    )(tiles)


def take_left(tiles, tile_rows):
    on_vmem = pl.BlockSpec(memory_space=pltpu.VMEM)
    return pl.pallas_call(
        left_kernel,
        in_specs=[on_vmem],
        out_specs=on_vmem,
        out_shape=jax.ShapeDtypeStruct(((NT - 2) * tile_rows, 2 * BLOCK), jnp.bfloat16),
        scratch_shapes=[pltpu.VMEM((tile_rows * NT // 2, BLOCK), jnp.float32)],
        compiler_params=pltpu.CompilerParams(vmem_limit_bytes=16 * 2**20),
        cost_estimate=pl.CostEstimate(
            flops=0, bytes_accessed=2 * NT * tile_rows * NT * BLOCK, transcendentals=0
        ),
    )(tiles)


def place_corner(place, slots, which, corner):
    row_index, column_index = place[0], place[1]
    chips, col_count, _, tile_rows, _ = slots[0].shape
    for core, held in enumerate(slots):
        for chip in range(chips):
            first_row = pl.multiple_of((row_index ^ (2 * chip + core)) * tile_rows, tile_rows)
            for col in range(col_count):
                first_col = pl.multiple_of((column_index ^ col) * BLOCK, BLOCK)
                corner[pl.ds(first_row, tile_rows), pl.ds(first_col, BLOCK)] = held[
                    chip, col, which
                ].astype(jnp.float32)


def own_tile(place, matrix, tile):
    tile_rows, tile_cols = tile.shape
    first_row = pl.multiple_of(place[0] * tile_rows, tile_rows)
    first_col = pl.multiple_of(place[1] * tile_cols, tile_cols)
    tile[...] = matrix[pl.ds(first_row, tile_rows), pl.ds(first_col, tile_cols)]


def first_kernel(place, near, far, own, side, inverse, rest, work, done, factor):
    place_corner(place, (near, far), 0, rest)
    factor_rest(rest, factor, inverse, work, done)
    own_tile(place, factor, own)
    order = rest.shape[0]
    for at, part in enumerate(split_three(inverse[...])):
        side[:, at * order : (at + 1) * order] = part


def second_kernel(
    place, near, far, first_side, own, side, inverse, cross, own_cross, rest, work, done, factor
):
    place_corner(place, (near, far), 0, rest)
    given = rest[...].astype(jnp.bfloat16)
    solved = fast_dot(beside([given] * 3), first_side[...], ((1,), (1,)))
    rest[...] = solved
    own_tile(place, rest, own_cross)
    solved = solved.astype(jnp.bfloat16)
    cross[...] = solved
    place_corner(place, (near, far), 1, rest)
    rest[...] = rest[...] - fast_dot(solved, solved, ((1,), (1,)))
    factor_rest(rest, factor, inverse, work, done)
    own_tile(place, factor, own)
    order = rest.shape[0]
    for at, part in enumerate(split_three(inverse[...])):
        side[:, at * order : (at + 1) * order] = part


def factor_call(body, place, slots, extra, out_shape, cost):
    on_vmem = pl.BlockSpec(memory_space=pltpu.VMEM)
    square = pltpu.VMEM((P_SIZE, P_SIZE), jnp.float32)
    return pl.pallas_call(
        body,
        in_specs=[pl.BlockSpec(memory_space=pltpu.SMEM)] + [on_vmem] * (2 + len(extra)),
        out_shape=out_shape,
        scratch_shapes=[*factor_scratch(), square],
        compiler_params=pltpu.CompilerParams(vmem_limit_bytes=20 * 2**20),
        cost_estimate=pl.CostEstimate(
            flops=cost, bytes_accessed=4 * 2**20, transcendentals=0
        ),
    )(place, *slots, *extra)


def rows_kernel(place, *refs):
    lefts = refs[:-9]
    first_inverse, second_inverse, cross, rounded, own, *scratch = refs[-9:]
    first_side, cross_side, second_side, solved_rows = scratch
    column_index = place[1]
    own_col = pl.multiple_of(column_index * BLOCK, BLOCK)
    order = P_SIZE

    @pl.when(pl.program_id(0) == 0)
    def _():
        for offset in range(len(lefts)):
            first = pl.multiple_of((column_index ^ offset) * BLOCK, BLOCK)
            here = pl.ds(first, BLOCK)
            to = [
                slice(k * order + offset * BLOCK, k * order + (offset + 1) * BLOCK)
                for k in range(3)
            ]
            for k, part in enumerate(split_three(first_inverse[:, here].T)):
                first_side[to[k], :] = part
            for k, part in enumerate(split_three(second_inverse[:, here].T)):
                second_side[to[k], :] = part
            cross_side[:, to[0]] = cross[here, :].astype(jnp.float32).T.astype(jnp.bfloat16)

    given = [left[:, 0:BLOCK] for left in lefts]
    solved = fast_dot(beside(given * 3), first_side[...])
    solved_rows[:, 0:order] = solved
    first_rounded = solved.astype(jnp.bfloat16)
    given = jnp.concatenate([left[:, BLOCK : 2 * BLOCK] for left in lefts], axis=1)
    left_over = given.astype(jnp.float32) - fast_dot(first_rounded, cross_side[...])
    high, middle, low = split_three(left_over)
    solved = (
        fast_dot(beside([high] * 3), second_side[...])
        + fast_dot(beside([middle] * 2), second_side[0 : 2 * order, :])
        + fast_dot(low, second_side[0:order, :])
    )
    solved_rows[:, order:] = solved
    rounded[:, 0:order] = first_rounded
    rounded[:, order:] = solved.astype(jnp.bfloat16)
    own[:, 0:BLOCK] = solved_rows[:, pl.ds(own_col, BLOCK)]
    own[:, BLOCK:] = solved_rows[:, pl.ds(order + own_col, BLOCK)]


def solve_rows(place, lefts, first_inverse, second_inverse, cross):
    count = lefts[0].shape[0]
    on_vmem = pl.BlockSpec(memory_space=pltpu.VMEM)
    return pl.pallas_call(
        rows_kernel,
        grid=(1,),
        in_specs=[pl.BlockSpec(memory_space=pltpu.SMEM)] + [on_vmem] * (len(lefts) + 3),
        out_shape=[
            jax.ShapeDtypeStruct((count, 2 * P_SIZE), jnp.bfloat16),
            jax.ShapeDtypeStruct((count, 2 * BLOCK), jnp.float32),
        ],
        scratch_shapes=[
            pltpu.VMEM((3 * P_SIZE, P_SIZE), jnp.bfloat16),
            pltpu.VMEM((P_SIZE, P_SIZE), jnp.bfloat16),
            pltpu.VMEM((3 * P_SIZE, P_SIZE), jnp.bfloat16),
            pltpu.VMEM((count, 2 * P_SIZE), jnp.float32),
        ],
        compiler_params=pltpu.CompilerParams(vmem_limit_bytes=24 * 2**20),
        cost_estimate=pl.CostEstimate(
            flops=12 * count * P_SIZE**2, bytes_accessed=10 * 2**20, transcendentals=0
        ),
    )(place, *lefts, first_inverse, second_inverse, cross)


def cols_kernel(chips, place, tiles, *refs):
    evens, odds = refs[:chips], refs[chips]
    first_own, first_side, second_own, second_side, cross, own_cross = refs[chips + 1 : chips + 7]
    rounded, own, result = refs[chips + 7 : chips + 10]
    given_cols, solved_cols, spread_rows, held, gone = refs[chips + 10 :]
    tile_rows = own_cross.shape[0]
    order = P_SIZE
    group = 4
    count = given_cols.shape[1]
    blank = jnp.zeros((tile_rows, BLOCK), jnp.float32)
    leaving = []

    def send(begin, end):
        for t in range(NT):
            here = (t, pl.ds(begin, end - begin))
            copy = pltpu.make_async_copy(held.at[here], result.at[here], gone.at[begin // 2, t])
            copy.start()
            leaving.append(copy)

    held[0, 0] = first_own[...]
    held[0, 1] = blank
    held[1, 0] = own_cross[...]
    held[1, 1] = second_own[...]
    for t in range(2, NT):
        rows = slice((t - 2) * tile_rows, (t - 1) * tile_rows)
        held[t, 0] = own[rows, 0:BLOCK]
        held[t, 1] = own[rows, BLOCK:]
    send(0, 2)
    for chip in range(chips):
        for core in range(2):
            source = odds.at[chip] if core else evens[chip]
            first = pl.multiple_of((place[0] ^ (2 * chip + core)) * tile_rows, tile_rows)
            for t in range(2):
                given_cols[pl.ds(t * order + first, tile_rows), :] = source[
                    t * tile_rows : (t + 1) * tile_rows, :
                ]
    for t in range(2, NT):
        natural_tile(tiles[t], spread_rows.at[t - 2], tile_rows)
    width = 1024
    for first_col in range(0, count, width):
        last_col = min(first_col + width, count)
        here = slice(first_col, last_col)
        given = given_cols[0:order, here]
        first = fast_dot(first_side[...], jnp.concatenate([given] * 3))
        first = first.astype(jnp.bfloat16)
        solved_cols[0:order, here] = first
        left_over = given_cols[order:, here].astype(jnp.float32) - fast_dot(cross[...], first)
        high, middle, low = split_three(left_over)
        second = (
            fast_dot(second_side[...], jnp.concatenate([high] * 3))
            + fast_dot(second_side[:, 0 : 2 * order], jnp.concatenate([middle] * 2))
            + fast_dot(second_side[:, 0:order], low)
        )
        solved_cols[order:, here] = second.astype(jnp.bfloat16)
        for begin in range(first_col, last_col, group * BLOCK):
            end = min(begin + group * BLOCK, last_col)
            product = fast_dot(rounded[...], solved_cols[:, begin:end])
            for column in range(begin, end, BLOCK):
                s = column // BLOCK + 2
                held[0, s] = blank
                held[1, s] = blank
                for t in range(2, NT):
                    rows = slice((t - 2) * tile_rows, (t - 1) * tile_rows)
                    held[t, s] = (
                        spread_rows[t - 2, pl.ds(s, tile_rows, stride=NT), :]
                        - product[rows, column - begin : column - begin + BLOCK]
                    )
            send(begin // BLOCK + 2, end // BLOCK + 2)
    for copy in leaving:
        copy.wait()


def solve_cols(place, tiles, evens, odds, corners, rounded, own, tile_rows):
    chips = len(evens)
    on_vmem = pl.BlockSpec(memory_space=pltpu.VMEM)
    shape = (NT, NT, tile_rows, BLOCK)
    solved = pltpu.VMEM((2 * P_SIZE, (NT - 2) * BLOCK), jnp.bfloat16)
    return pl.pallas_call(
        functools.partial(cols_kernel, chips),
        in_specs=[pl.BlockSpec(memory_space=pltpu.SMEM)] + [on_vmem] * (chips + len(corners) + 4),
        out_specs=pl.BlockSpec(memory_space=pl.ANY),
        out_shape=jax.ShapeDtypeStruct(shape, jnp.float32),
        scratch_shapes=[
            solved,
            solved,
            pltpu.VMEM((NT - 2, NT * tile_rows, BLOCK), jnp.float32),
            pltpu.VMEM(shape, jnp.float32),
            pltpu.SemaphoreType.DMA((NT // 2, NT)),
        ],
        compiler_params=pltpu.CompilerParams(vmem_limit_bytes=44 * 2**20),
        cost_estimate=pl.CostEstimate(
            flops=10 * 10**9, bytes_accessed=24 * 2**20, transcendentals=0
        ),
    )(place, tiles, *evens, odds, *corners, rounded, own)


def swap(value, axis, offset):
    count = lax.axis_size(axis)
    return lax.ppermute(value, axis, [(i, i ^ offset) for i in range(count)])


def per_device(kernel):
    row_count = lax.axis_size("row")
    col_count = lax.axis_size("col")
    tile_rows = P_SIZE // row_count
    if P_SIZE != col_count * BLOCK or tile_rows % STEP:
        return per_device_general(kernel)
    place = jnp.stack([lax.axis_index("row"), lax.axis_index("col")]).astype(jnp.int32)
    tiles = kernel.reshape(NT, NT, tile_rows * BLOCK)
    corner, top = take_top(tiles[0:2], tile_rows)
    left = take_left(tiles, tile_rows)
    chips = range(2, row_count, 2)
    over_cols = jnp.stack([corner] + [swap(corner, "col", d) for d in range(1, col_count)])
    over_cols, left = lax.optimization_barrier((over_cols, left))
    first = over_cols[:, 0:1]
    near = jnp.stack([first] + [swap(first, "row", d) for d in chips])
    lefts = {0: left}
    for d in range(1, col_count):
        if d != 2:
            lefts[d] = swap(left, "col", d)
    near, other = lax.optimization_barrier((near, over_cols[:, 1:]))
    far = swap(near, "row", 1)
    other_near = [other] + [swap(other, "row", d) for d in chips]
    tile = jax.ShapeDtypeStruct((tile_rows, BLOCK), jnp.float32)
    square = jax.ShapeDtypeStruct((P_SIZE, P_SIZE), jnp.float32)
    first_own, first_side, first_inverse = factor_call(
        first_kernel,
        place,
        (near, far),
        (),
        [tile, jax.ShapeDtypeStruct((P_SIZE, 3 * P_SIZE), jnp.bfloat16), square],
        40 * 10**9,
    )
    others = [lefts[d] for d in sorted(lefts) if d]
    *other_near, top, left, first_side = lax.optimization_barrier(
        (*other_near, top, left, first_side, *others)
    )[: len(other_near) + 3]
    other_near = jnp.stack(other_near)
    other_far = swap(other_near, "row", 1)
    if col_count > 2:
        lefts[2] = swap(left, "col", 2)
    lefts = [lefts[d] for d in range(col_count)]
    evens = [top] + [swap(top, "row", d) for d in chips]
    second_own, second_side, second_inverse, cross, own_cross = factor_call(
        second_kernel,
        place,
        (other_near, other_far),
        (first_side,),
        [
            tile,
            jax.ShapeDtypeStruct((P_SIZE, 3 * P_SIZE), jnp.bfloat16),
            square,
            jax.ShapeDtypeStruct((P_SIZE, P_SIZE), jnp.bfloat16),
            tile,
        ],
        40 * 10**9,
    )
    *evens, second_side, lefts[2 % col_count] = lax.optimization_barrier(
        (*evens, second_side, lefts[2 % col_count])
    )
    odds = swap(jnp.stack(evens), "row", 1)
    rounded, own = solve_rows(place, lefts, first_inverse, second_inverse, cross)
    corners = (first_own, first_side, second_own, second_side, cross, own_cross)
    result = solve_cols(place, tiles, evens, odds, corners, rounded, own, tile_rows)
    return result.reshape(kernel.shape)


def solution(mesh):
    placed = P(None, "row", None, "col", None)
    return jax.shard_map(
        per_device, mesh=mesh, in_specs=(placed,), out_specs=placed, check_vma=False
    )
```

profile of v0, /device:TPU:1, one launch (start us, length us, event | category | flops | bytes accessed | tf_op | source)
XLA Modules:
  0.0 96.9 jit_solution(8190135154941220098)
XLA Ops:
  0.0 1.1 %slice_bitcast_fusion.tiles = bf16[2,16,8192]{2,1,0:T(8,128)(2,1)S(1)} fusion(bf16[16,1,16,1,8192]{4,2,0,3,1:T(8,128)(2,1)} %bitcast.28), kind=kLoop, calls=%fused_computation.1 | loop fusion | bytes 1048576 | tf_op jit(solution)/shard_map/slice | solution.py:553
  1.1 0.4 shard_map.17
  1.5 4.2 %collective-permute-start.2 = (bf16[3,64,128]{2,1,0:T(8,128)(2,1)S(1)}, bf16[3,64,128]{2,1,0:T(8,128)(2,1)S(1)}, u32[]{:S(2)}, u32[]{:S(2)}) collective-permute-start(bf16[3,64,128]{2,1,0:T(8,128)(2,1)S(1)} %get-tuple-element.34), channel_id=1, source_target_pairs={{0,3},{1,2},{2,1},{3,0},{4,7},{5,6},{6,5},{7,4},{8,11},{9,10},{10,... | collective-permute-start | bytes 147464 | tf_op jit(solution)/shard_map/ppermute | solution.py:542
  6.1 2.2 %copy-done = bf16[16,1,16,1,8192]{4,2,3,1,0:T(8,128)(2,1)S(1)} copy-done((bf16[16,1,16,1,8192]{4,2,3,1,0:T(8,128)(2,1)S(1)}, bf16[16,1,16,1,8192]{4,2,3,1,0:T(8,128)(2,1)}, u32[]{:S(2)}) %copy-start) | copy-done | bytes 4194328
  8.6 1.5 %collective-permute-done.1 = bf16[3,64,128]{2,1,0:T(8,128)(2,1)S(1)} collective-permute-done((bf16[3,64,128]{2,1,0:T(8,128)(2,1)S(1)}, bf16[3,64,128]{2,1,0:T(8,128)(2,1)S(1)}, u32[]{:S(2)}, u32[]{:S(2)}) %collective-permute-start.1) | collective-permute-done | bytes 49184 | tf_op jit(solution)/shard_map/ppermute | solution.py:542
  10.1 2.2 %collective-permute-start.5 = (bf16[4,1,64,128]{3,2,1,0:T(8,128)(2,1)S(1)}, bf16[4,1,64,128]{3,2,1,0:T(8,128)(2,1)S(1)}, u32[]{:S(2)}, u32[]{:S(2)}) collective-permute-start(bf16[4,1,64,128]{3,2,1,0:T(8,128)(2,1)S(1)} %get-tuple-element.65), channel_id=1, source_target_pairs={{0,24},{4,28},{8,16},{12,20},{16,8},{20,12},{24,0},{28,4},{1,25},{... | collective-permute-start | bytes 196616 | tf_op jit(solution)/shard_map/ppermute | solution.py:542
  12.9 1.4 %collective-permute-done.5 = bf16[4,1,64,128]{3,2,1,0:T(8,128)(2,1)S(1)} collective-permute-done((bf16[4,1,64,128]{3,2,1,0:T(8,128)(2,1)S(1)}, bf16[4,1,64,128]{3,2,1,0:T(8,128)(2,1)S(1)}, u32[]{:S(2)}, u32[]{:S(2)}) %collective-permute-start.5) | collective-permute-done | bytes 65568 | tf_op jit(solution)/shard_map/ppermute | solution.py:542
  14.2 1.3 %collective-permute-done.4 = bf16[4,1,64,128]{3,2,0,1:T(8,128)(2,1)S(1)} collective-permute-done((bf16[4,1,64,128]{3,2,0,1:T(8,128)(2,1)S(1)}, bf16[4,1,64,128]{3,2,0,1:T(8,128)(2,1)S(1)}, u32[]{:S(2)}, u32[]{:S(2)}) %collective-permute-start.4) | collective-permute-done | bytes 65568 | tf_op jit(solution)/shard_map/ppermute | solution.py:542
  15.5 0.7 collective-permute-done.3
  16.2 2.9 %collective-permute-start.9 = (bf16[4,4,1,64,128]{4,3,1,2,0:T(8,128)(2,1)S(1)}, bf16[4,4,1,64,128]{4,3,1,2,0:T(8,128)(2,1)S(1)}, u32[]{:S(2)}, u32[]{:S(2)}) collective-permute-start(bf16[4,4,1,64,128]{4,3,1,2,0:T(8,128)(2,1)S(1)} %pad_maximum_fusion.2), channel_id=1, source_target_pairs={{0,4},{4,0},{8,12},{12,8},{16,20},{20,16},{24,28},{28,24},{1,5},{5... | collective-permute-start | bytes 786440 | tf_op jit(solution)/shard_map/ppermute | solution.py:542
  19.2 1.8 %collective-permute-start.11 = (bf16[896,256]{1,0:T(8,128)(2,1)S(1)}, bf16[896,256]{1,0:T(8,128)(2,1)S(1)}, u32[]{:S(2)}, u32[]{:S(2)}) collective-permute-start(bf16[896,256]{1,0:T(8,128)(2,1)S(1)} %shard_map.18.refs_0_), channel_id=1, source_target_pairs={{0,3},{1,2},{2,1},{3,0},{4,7},{5,6},{6,5},{7,4},{8,11},{9,10},{10,... | collective-permute-start | bytes 1376264 | tf_op jit(solution)/shard_map/ppermute | solution.py:542
  21.2 1.2 %collective-permute-start.8 = (bf16[4,2,64,128]{3,2,1,0:T(8,128)(2,1)S(1)}, bf16[4,2,64,128]{3,2,1,0:T(8,128)(2,1)S(1)}, u32[]{:S(2)}, u32[]{:S(2)}) collective-permute-start(bf16[4,2,64,128]{3,2,1,0:T(8,128)(2,1)S(1)} %slice.15), channel_id=1, source_target_pairs={{0,24},{4,28},{8,16},{12,20},{16,8},{20,12},{24,0},{28,4},{1,25},{... | collective-permute-start | bytes 393224 | tf_op jit(solution)/shard_map/ppermute | solution.py:542
  22.6 1.2 %collective-permute-start.6 = (bf16[4,2,64,128]{3,2,1,0:T(8,128)(2,1)S(1)}, bf16[4,2,64,128]{3,2,1,0:T(8,128)(2,1)S(1)}, u32[]{:S(2)}, u32[]{:S(2)}) collective-permute-start(bf16[4,2,64,128]{3,2,1,0:T(8,128)(2,1)S(1)} %slice.15), channel_id=1, source_target_pairs={{0,8},{4,12},{8,0},{12,4},{16,24},{20,28},{24,16},{28,20},{1,9},{5... | collective-permute-start | bytes 393224 | tf_op jit(solution)/shard_map/ppermute | solution.py:542
  23.9 18.0 %shard_map.19 = (f32[64,128]{1,0:T(8,128)S(1)}, bf16[512,1536]{1,0:T(8,128)(2,1)S(1)}, f32[512,512]{1,0:T(8,128)S(1)}) custom-call(s32[2]{0:T(128)S(1)} %pad_add_fusion.place, bf16[4,4,1,64,128]{4,3,2,1,0:T(8,128)(2,1)S(1)} %bitcast.35, bf16[4,4,1,64,128]{4,3,2,1,0:T(8,128)(2,1)S(1)} %bitcast.37), custom_call_target="tpu_custom_call" | custom-call | flops 40000000000 | bytes 4194304 | tf_op jit(solution)/shard_map/pallas_call | solution.py:366
  41.9 1.3 %collective-permute-done.10.refs_1_ = bf16[896,256]{1,0:T(8,128)(2,1)S(1)} collective-permute-done((bf16[896,256]{1,0:T(8,128)(2,1)S(1)}, bf16[896,256]{1,0:T(8,128)(2,1)S(1)}, u32[]{:S(2)}, u32[]{:S(2)}) %collective-permute-start.10) | collective-permute-done | bytes 458784 | tf_op jit(solution)/shard_map/ppermute | solution.py:542
  43.2 0.6 collective-permute-start.15
  43.9 1.2 %collective-permute-start.14 = (bf16[128,1792]{1,0:T(8,128)(2,1)S(1)}, bf16[128,1792]{1,0:T(8,128)(2,1)S(1)}, u32[]{:S(2)}, u32[]{:S(2)}) collective-permute-start(bf16[128,1792]{1,0:T(8,128)(2,1)S(1)} %get-tuple-element.49.refs_0_), channel_id=1, source_target_pairs={{0,24},{4,28},{8,16},{12,20},{16,8},{20,12},{24,0},{28,4},{1,25},{... | collective-permute-start | bytes 1376264 | tf_op jit(solution)/shard_map/ppermute | solution.py:542
  45.3 1.2 %collective-permute-start.12 = (bf16[128,1792]{1,0:T(8,128)(2,1)S(1)}, bf16[128,1792]{1,0:T(8,128)(2,1)S(1)}, u32[]{:S(2)}, u32[]{:S(2)}) collective-permute-start(bf16[128,1792]{1,0:T(8,128)(2,1)S(1)} %get-tuple-element.49.refs_0_), channel_id=1, source_target_pairs={{0,8},{4,12},{8,0},{12,4},{16,24},{20,28},{24,16},{28,20},{1,9},{5... | collective-permute-start | bytes 1376264 | tf_op jit(solution)/shard_map/ppermute | solution.py:542
  46.6 1.1 %collective-permute-start.16 = (bf16[896,256]{1,0:T(8,128)(2,1)S(1)}, bf16[896,256]{1,0:T(8,128)(2,1)S(1)}, u32[]{:S(2)}, u32[]{:S(2)}) collective-permute-start(bf16[896,256]{1,0:T(8,128)(2,1)S(1)} %shard_map.18.refs_0_), channel_id=1, source_target_pairs={{0,2},{1,3},{2,0},{3,1},{4,6},{5,7},{6,4},{7,5},{8,10},{9,11},{10,... | collective-permute-start | bytes 1376264 | tf_op jit(solution)/shard_map/ppermute | solution.py:542
  47.6 19.6 %shard_map.20 = (f32[64,128]{1,0:T(8,128)S(1)}, bf16[512,1536]{1,0:T(8,128)(2,1)S(1)}, f32[512,512]{1,0:T(8,128)S(1)}, bf16[512,512]{1,0:T(8,128)(2,1)S(1)}, f32[64,128]{1,0:T(8,128)S(1)}) custom-call(s32[2]{0:T(128)S(1)} %pad_add_fusion.place, bf16[4,4,2,64,128]{4,3,2,1,0:T(8,128)(2,1)S(1)} %pad_maximum_fusion.1.near, ...), custom_call_target="tpu_custom_call" | custom-call | flops 40000000000 | bytes 4194304 | tf_op jit(solution)/shard_map/pallas_call | solution.py:366
  67.2 1.9 %collective-permute-done.16.refs_2_ = bf16[896,256]{1,0:T(8,128)(2,1)S(1)} collective-permute-done((bf16[896,256]{1,0:T(8,128)(2,1)S(1)}, bf16[896,256]{1,0:T(8,128)(2,1)S(1)}, u32[]{:S(2)}, u32[]{:S(2)}) %collective-permute-start.16) | collective-permute-done | bytes 458784 | tf_op jit(solution)/shard_map/ppermute | solution.py:542
  69.4 1.2 %collective-permute-start.17 = (bf16[4,128,1792]{2,1,0:T(8,128)(2,1)S(1)}, bf16[4,128,1792]{2,1,0:T(8,128)(2,1)S(1)}, u32[]{:S(2)}, u32[]{:S(2)}) collective-permute-start(bf16[4,128,1792]{2,1,0:T(8,128)(2,1)S(1)} %pad_maximum_fusion), channel_id=1, source_target_pairs={{0,4},{4,0},{8,12},{12,8},{16,20},{20,16},{24,28},{28,24},{1,5},{5... | collective-permute-start | bytes 5505032 | tf_op jit(solution)/shard_map/ppermute | solution.py:542
  70.5 5.9 %shard_map.21 = (bf16[896,1024]{1,0:T(8,128)(2,1)S(1)}, f32[896,256]{1,0:T(8,128)S(1)}) custom-call(s32[2]{0:T(128)S(1)} %pad_add_fusion.place, bf16[896,256]{1,0:T(8,128)(2,1)S(1)} %shard_map.18.refs_0_, bf16[896,256]{1,0:T(8,128)(2,1)S(1)} %collective-permute-done.10.refs_1_, bf16[896,256]{1,0:T(8,128)(2,1)S(1)} %collective-permute-done.16.refs_2_, ...), custom_call_target="tpu_custom_call" | custom-call | flops 2818572288 | bytes 10485760 | tf_op jit(solution)/shard_map/pallas_call | solution.py:423
  76.4 20.3 %shard_map.22 = f32[16,16,64,128]{3,2,1,0:T(8,128)} custom-call(s32[2]{0:T(128)S(1)} %pad_add_fusion.place, bf16[16,16,8192]{2,1,0:T(8,128)(2,1)} %bitcast.29, bf16[128,1792]{1,0:T(8,128)(2,1)S(1)} %get-tuple-element.49.refs_0_, bf16[128,1792]{1,0:T(8,128)(2,1)S(1)} %collective-permute-done.12.refs_1_, ...), custom_call_target="tpu_custom_call" | custom-call | flops 10000000000 | bytes 25165824 | tf_op jit(solution)/shard_map/pallas_call | solution.py:521
  (28 shorter events, 2.4 us)
Async XLA Ops:
  1.5 7.1 %collective-permute-start.2 = (bf16[3,64,128]{2,1,0:T(8,128)(2,1)S(1)}, bf16[3,64,128]{2,1,0:T(8,128)(2,1)S(1)}, u32[]{:S(2)}, u32[]{:S(2)}) collective-permute-start(bf16[3,64,128]{2,1,0:T(8,128)(2,1)S(1)} %get-tuple-element.34), channel_id=1, source_target_pairs={{0,3},{1,2},{2,1},{3,0},{4,7},{5,6},{6,5},{7,4},{8,11},{9,10},{10,... | collective-permute-start | bytes 147464 | tf_op jit(solution)/shard_map/ppermute | solution.py:542
  5.7 4.4 %collective-permute-start.1 = (bf16[3,64,128]{2,1,0:T(8,128)(2,1)S(1)}, bf16[3,64,128]{2,1,0:T(8,128)(2,1)S(1)}, u32[]{:S(2)}, u32[]{:S(2)}) collective-permute-start(bf16[3,64,128]{2,1,0:T(8,128)(2,1)S(1)} %get-tuple-element.34), channel_id=1, source_target_pairs={{0,2},{1,3},{2,0},{3,1},{4,6},{5,7},{6,4},{7,5},{8,10},{9,11},{10,... | collective-permute-start | bytes 147464 | tf_op jit(solution)/shard_map/ppermute | solution.py:542
  5.7 4.4 %collective-permute-start = (bf16[3,64,128]{2,1,0:T(8,128)(2,1)S(1)}, bf16[3,64,128]{2,1,0:T(8,128)(2,1)S(1)}, u32[]{:S(2)}, u32[]{:S(2)}) collective-permute-start(bf16[3,64,128]{2,1,0:T(8,128)(2,1)S(1)} %get-tuple-element.34), channel_id=1, source_target_pairs={{0,1},{1,0},{2,3},{3,2},{4,5},{5,4},{6,7},{7,6},{8,9},{9,8},{10,11... | collective-permute-start | bytes 147464 | tf_op jit(solution)/shard_map/ppermute | solution.py:542
  6.1 2.2 %copy-start = (bf16[16,1,16,1,8192]{4,2,3,1,0:T(8,128)(2,1)S(1)}, bf16[16,1,16,1,8192]{4,2,3,1,0:T(8,128)(2,1)}, u32[]{:S(2)}) copy-start(bf16[16,1,16,1,8192]{4,2,3,1,0:T(8,128)(2,1)} %param.1) | copy-start | bytes 12582916
  10.1 4.1 %collective-permute-start.5 = (bf16[4,1,64,128]{3,2,1,0:T(8,128)(2,1)S(1)}, bf16[4,1,64,128]{3,2,1,0:T(8,128)(2,1)S(1)}, u32[]{:S(2)}, u32[]{:S(2)}) collective-permute-start(bf16[4,1,64,128]{3,2,1,0:T(8,128)(2,1)S(1)} %get-tuple-element.65), channel_id=1, source_target_pairs={{0,24},{4,28},{8,16},{12,20},{16,8},{20,12},{24,0},{28,4},{1,25},{... | collective-permute-start | bytes 196616 | tf_op jit(solution)/shard_map/ppermute | solution.py:542
  12.4 3.1 %collective-permute-start.4 = (bf16[4,1,64,128]{3,2,0,1:T(8,128)(2,1)S(1)}, bf16[4,1,64,128]{3,2,0,1:T(8,128)(2,1)S(1)}, u32[]{:S(2)}, u32[]{:S(2)}) collective-permute-start(bf16[4,1,64,128]{3,2,0,1:T(8,128)(2,1)S(1)} %get-tuple-element.64), channel_id=1, source_target_pairs={{0,16},{4,20},{8,24},{12,28},{16,0},{20,4},{24,8},{28,12},{1,17},{... | collective-permute-start | bytes 196616 | tf_op jit(solution)/shard_map/ppermute | solution.py:542
  12.6 3.6 %collective-permute-start.3 = (bf16[4,1,64,128]{3,2,0,1:T(8,128)(2,1)S(1)}, bf16[4,1,64,128]{3,2,0,1:T(8,128)(2,1)S(1)}, u32[]{:S(2)}, u32[]{:S(2)}) collective-permute-start(bf16[4,1,64,128]{3,2,0,1:T(8,128)(2,1)S(1)} %get-tuple-element.64), channel_id=1, source_target_pairs={{0,8},{4,12},{8,0},{12,4},{16,24},{20,28},{24,16},{28,20},{1,9},{5... | collective-permute-start | bytes 196616 | tf_op jit(solution)/shard_map/ppermute | solution.py:542
  16.2 6.4 %collective-permute-start.9 = (bf16[4,4,1,64,128]{4,3,1,2,0:T(8,128)(2,1)S(1)}, bf16[4,4,1,64,128]{4,3,1,2,0:T(8,128)(2,1)S(1)}, u32[]{:S(2)}, u32[]{:S(2)}) collective-permute-start(bf16[4,4,1,64,128]{4,3,1,2,0:T(8,128)(2,1)S(1)} %pad_maximum_fusion.2), channel_id=1, source_target_pairs={{0,4},{4,0},{8,12},{12,8},{16,20},{20,16},{24,28},{28,24},{1,5},{5... | collective-permute-start | bytes 786440 | tf_op jit(solution)/shard_map/ppermute | solution.py:542
  19.2 22.7 %collective-permute-start.11 = (bf16[896,256]{1,0:T(8,128)(2,1)S(1)}, bf16[896,256]{1,0:T(8,128)(2,1)S(1)}, u32[]{:S(2)}, u32[]{:S(2)}) collective-permute-start(bf16[896,256]{1,0:T(8,128)(2,1)S(1)} %shard_map.18.refs_0_), channel_id=1, source_target_pairs={{0,3},{1,2},{2,1},{3,0},{4,7},{5,6},{6,5},{7,4},{8,11},{9,10},{10,... | collective-permute-start | bytes 1376264 | tf_op jit(solution)/shard_map/ppermute | solution.py:542
  21.0 22.2 %collective-permute-start.10 = (bf16[896,256]{1,0:T(8,128)(2,1)S(1)}, bf16[896,256]{1,0:T(8,128)(2,1)S(1)}, u32[]{:S(2)}, u32[]{:S(2)}) collective-permute-start(bf16[896,256]{1,0:T(8,128)(2,1)S(1)} %shard_map.18.refs_0_), channel_id=1, source_target_pairs={{0,1},{1,0},{2,3},{3,2},{4,5},{5,4},{6,7},{7,6},{8,9},{9,8},{10,11... | collective-permute-start | bytes 1376264 | tf_op jit(solution)/shard_map/ppermute | solution.py:542
  21.2 20.6 %collective-permute-start.8 = (bf16[4,2,64,128]{3,2,1,0:T(8,128)(2,1)S(1)}, bf16[4,2,64,128]{3,2,1,0:T(8,128)(2,1)S(1)}, u32[]{:S(2)}, u32[]{:S(2)}) collective-permute-start(bf16[4,2,64,128]{3,2,1,0:T(8,128)(2,1)S(1)} %slice.15), channel_id=1, source_target_pairs={{0,24},{4,28},{8,16},{12,20},{16,8},{20,12},{24,0},{28,4},{1,25},{... | collective-permute-start | bytes 393224 | tf_op jit(solution)/shard_map/ppermute | solution.py:542
  22.4 19.4 %collective-permute-start.7 = (bf16[4,2,64,128]{3,2,1,0:T(8,128)(2,1)S(1)}, bf16[4,2,64,128]{3,2,1,0:T(8,128)(2,1)S(1)}, u32[]{:S(2)}, u32[]{:S(2)}) collective-permute-start(bf16[4,2,64,128]{3,2,1,0:T(8,128)(2,1)S(1)} %slice.15), channel_id=1, source_target_pairs={{0,16},{4,20},{8,24},{12,28},{16,0},{20,4},{24,8},{28,12},{1,17},{... | collective-permute-start | bytes 393224 | tf_op jit(solution)/shard_map/ppermute | solution.py:542
  22.6 19.2 %collective-permute-start.6 = (bf16[4,2,64,128]{3,2,1,0:T(8,128)(2,1)S(1)}, bf16[4,2,64,128]{3,2,1,0:T(8,128)(2,1)S(1)}, u32[]{:S(2)}, u32[]{:S(2)}) collective-permute-start(bf16[4,2,64,128]{3,2,1,0:T(8,128)(2,1)S(1)} %slice.15), channel_id=1, source_target_pairs={{0,8},{4,12},{8,0},{12,4},{16,24},{20,28},{24,16},{28,20},{1,9},{5... | collective-permute-start | bytes 393224 | tf_op jit(solution)/shard_map/ppermute | solution.py:542
  43.2 4.4 %collective-permute-start.15 = (bf16[4,4,2,64,128]{4,3,2,1,0:T(8,128)(2,1)S(1)}, bf16[4,4,2,64,128]{4,3,2,1,0:T(8,128)(2,1)S(1)}, u32[]{:S(2)}, u32[]{:S(2)}) collective-permute-start(bf16[4,4,2,64,128]{4,3,2,1,0:T(8,128)(2,1)S(1)} %pad_maximum_fusion.1.near), channel_id=1, source_target_pairs={{0,4},{4,0},{8,12},{12,8},{16,20},{20,16},{24,28},{28,24},{1,5},{5... | collective-permute-start | bytes 1572872 | tf_op jit(solution)/shard_map/ppermute | solution.py:542
  43.9 25.2 %collective-permute-start.14 = (bf16[128,1792]{1,0:T(8,128)(2,1)S(1)}, bf16[128,1792]{1,0:T(8,128)(2,1)S(1)}, u32[]{:S(2)}, u32[]{:S(2)}) collective-permute-start(bf16[128,1792]{1,0:T(8,128)(2,1)S(1)} %get-tuple-element.49.refs_0_), channel_id=1, source_target_pairs={{0,24},{4,28},{8,16},{12,20},{16,8},{20,12},{24,0},{28,4},{1,25},{... | collective-permute-start | bytes 1376264 | tf_op jit(solution)/shard_map/ppermute | solution.py:542
  45.1 24.0 %collective-permute-start.13 = (bf16[128,1792]{1,0:T(8,128)(2,1)S(1)}, bf16[128,1792]{1,0:T(8,128)(2,1)S(1)}, u32[]{:S(2)}, u32[]{:S(2)}) collective-permute-start(bf16[128,1792]{1,0:T(8,128)(2,1)S(1)} %get-tuple-element.49.refs_0_), channel_id=1, source_target_pairs={{0,16},{4,20},{8,24},{12,28},{16,0},{20,4},{24,8},{28,12},{1,17},{... | collective-permute-start | bytes 1376264 | tf_op jit(solution)/shard_map/ppermute | solution.py:542
  45.3 23.8 %collective-permute-start.12 = (bf16[128,1792]{1,0:T(8,128)(2,1)S(1)}, bf16[128,1792]{1,0:T(8,128)(2,1)S(1)}, u32[]{:S(2)}, u32[]{:S(2)}) collective-permute-start(bf16[128,1792]{1,0:T(8,128)(2,1)S(1)} %get-tuple-element.49.refs_0_), channel_id=1, source_target_pairs={{0,8},{4,12},{8,0},{12,4},{16,24},{20,28},{24,16},{28,20},{1,9},{5... | collective-permute-start | bytes 1376264 | tf_op jit(solution)/shard_map/ppermute | solution.py:542
  46.6 22.6 %collective-permute-start.16 = (bf16[896,256]{1,0:T(8,128)(2,1)S(1)}, bf16[896,256]{1,0:T(8,128)(2,1)S(1)}, u32[]{:S(2)}, u32[]{:S(2)}) collective-permute-start(bf16[896,256]{1,0:T(8,128)(2,1)S(1)} %shard_map.18.refs_0_), channel_id=1, source_target_pairs={{0,2},{1,3},{2,0},{3,1},{4,6},{5,7},{6,4},{7,5},{8,10},{9,11},{10,... | collective-permute-start | bytes 1376264 | tf_op jit(solution)/shard_map/ppermute | solution.py:542
  69.4 7.1 %collective-permute-start.17 = (bf16[4,128,1792]{2,1,0:T(8,128)(2,1)S(1)}, bf16[4,128,1792]{2,1,0:T(8,128)(2,1)S(1)}, u32[]{:S(2)}, u32[]{:S(2)}) collective-permute-start(bf16[4,128,1792]{2,1,0:T(8,128)(2,1)S(1)} %pad_maximum_fusion), channel_id=1, source_target_pairs={{0,4},{4,0},{8,12},{12,8},{16,20},{20,16},{24,28},{28,24},{1,5},{5... | collective-permute-start | bytes 5505032 | tf_op jit(solution)/shard_map/ppermute | solution.py:542
where the time goes:
time: 97.1 us; the launch traced here: 96.9 us
  Pallas kernels  64.5 us (66%)
  starting transfers between devices  20.4 us (21%)
  waiting for transfers between devices  8 us (8%)
  local copies, waits for them, and re-layouts  3.3 us (3%)
    pallas_call x2, Pallas kernels, factor_call(): pl.pallas_call(body, in_specs=[pl.BlockSpec(memory_space=pltpu.SMEM)] + [...  37.5 us
    ppermute x18, starting transfers between devices, swap(): return lax.ppermute(value, axis, [(i, i ^ offset) for i in range(count)])  20.4 us
    pallas_call x1, Pallas kernels, solve_cols(): pl.pallas_call(functools.partial(cols_kernel, chips), in_specs=[pl.BlockS...  20.3 us
    ppermute x18, waiting for transfers between devices, swap(): return lax.ppermute(value, axis, [(i, i ^ offset) for i in range(count)])  8 us
    pallas_call x1, Pallas kernels, solve_rows(): pl.pallas_call(rows_kernel, grid=(1,), in_specs=[pl.BlockSpec(memory_spac...  5.88 us
    unnamed x2, local copies, waits for them, and re-layouts  2.19 us
  transfers between devices with their start and end apart: 18, of which 6 were waited for; matrix products, arithmetic and copies ran while one was open for 0% of the time, Pallas kernels for 45%

commit v1 on v0

--- a/solution.py
+++ b/solution.py
@@ -441,6 +441,15 @@
     )(place, *lefts, first_inverse, second_inverse, cross)
 
 
+def lower_dot(side, parts):
+    order = side.shape[0]
+    half = order // 2
+    corner = beside([side[0:half, k * order : k * order + half] for k in range(len(parts))])
+    upper = fast_dot(corner, jnp.concatenate([part[0:half] for part in parts]))
+    lower = fast_dot(side[half:order, 0 : len(parts) * order], jnp.concatenate(parts))
+    return jnp.concatenate([upper, lower])
+
+
 def cols_kernel(chips, place, tiles, *refs):
     evens, odds = refs[:chips], refs[chips]
     first_own, first_side, second_own, second_side, cross, own_cross = refs[chips + 1 : chips + 7]
@@ -484,15 +493,14 @@
         last_col = min(first_col + width, count)
         here = slice(first_col, last_col)
         given = given_cols[0:order, here]
-        first = fast_dot(first_side[...], jnp.concatenate([given] * 3))
-        first = first.astype(jnp.bfloat16)
+        first = lower_dot(first_side, [given] * 3).astype(jnp.bfloat16)
         solved_cols[0:order, here] = first
         left_over = given_cols[order:, here].astype(jnp.float32) - fast_dot(cross[...], first)
         high, middle, low = split_three(left_over)
         second = (
-            fast_dot(second_side[...], jnp.concatenate([high] * 3))
-            + fast_dot(second_side[:, 0 : 2 * order], jnp.concatenate([middle] * 2))
-            + fast_dot(second_side[:, 0:order], low)
+            lower_dot(second_side, [high] * 3)
+            + lower_dot(second_side, [middle] * 2)
+            + lower_dot(second_side, [low])
         )
         solved_cols[order:, here] = second.astype(jnp.bfloat16)
         for begin in range(first_col, last_col, group * BLOCK):

time: 97.1 us -> 94.4 us (0.972)
  Pallas kernels: 64.5 us -> 61.8 us
    pallas_call x1, Pallas kernels: 20.3 us -> 17.6 us  [solve_cols(): pl.pallas_call(functools.partial(cols_kernel, chips), in_specs=[pl.BlockS...]
  transfers between devices with their start and end apart: 18 -> 18, of which waited for: 6 -> 6; matrix products, arithmetic and copies ran while one was open for 0% -> 0% of each run, Pallas kernels for 45% -> 46%
where the time goes in v1:
time: 94.4 us; the launch traced here: 94.2 us
  Pallas kernels  61.8 us (65%)
  starting transfers between devices  20.4 us (22%)
  waiting for transfers between devices  8 us (8%)
  local copies, waits for them, and re-layouts  3.3 us (3%)
    pallas_call x2, Pallas kernels, factor_call(): pl.pallas_call(body, in_specs=[pl.BlockSpec(memory_space=pltpu.SMEM)] + [...  37.5 us
    ppermute x18, starting transfers between devices, swap(): return lax.ppermute(value, axis, [(i, i ^ offset) for i in range(count)])  20.4 us
    pallas_call x1, Pallas kernels, solve_cols(): pl.pallas_call(functools.partial(cols_kernel, chips), in_specs=[pl.BlockS...  17.6 us
    ppermute x18, waiting for transfers between devices, swap(): return lax.ppermute(value, axis, [(i, i ^ offset) for i in range(count)])  8 us
    pallas_call x1, Pallas kernels, solve_rows(): pl.pallas_call(rows_kernel, grid=(1,), in_specs=[pl.BlockSpec(memory_spac...  5.88 us
    unnamed x2, local copies, waits for them, and re-layouts  2.19 us
  transfers between devices with their start and end apart: 18, of which 6 were waited for; matrix products, arithmetic and copies ran while one was open for 0% of the time, Pallas kernels for 46%

profile of v1, /device:TPU:1, one launch (start us, length us, event | category | flops | bytes accessed | tf_op | source)
XLA Modules:
  0.0 94.2 jit_solution(9791046483253639434)
XLA Ops:
  0.0 1.1 %slice_bitcast_fusion.tiles = bf16[2,16,8192]{2,1,0:T(8,128)(2,1)S(1)} fusion(bf16[16,1,16,1,8192]{4,2,0,3,1:T(8,128)(2,1)} %bitcast.28), kind=kLoop, calls=%fused_computation.1 | loop fusion | bytes 1048576 | tf_op jit(solution)/shard_map/slice | solution.py:561
  1.1 0.4 shard_map.17
  1.5 4.2 %collective-permute-start.2 = (bf16[3,64,128]{2,1,0:T(8,128)(2,1)S(1)}, bf16[3,64,128]{2,1,0:T(8,128)(2,1)S(1)}, u32[]{:S(2)}, u32[]{:S(2)}) collective-permute-start(bf16[3,64,128]{2,1,0:T(8,128)(2,1)S(1)} %get-tuple-element.34), channel_id=1, source_target_pairs={{0,3},{1,2},{2,1},{3,0},{4,7},{5,6},{6,5},{7,4},{8,11},{9,10},{10,... | collective-permute-start | bytes 147464 | tf_op jit(solution)/shard_map/ppermute | solution.py:550
  6.1 2.2 %copy-done = bf16[16,1,16,1,8192]{4,2,3,1,0:T(8,128)(2,1)S(1)} copy-done((bf16[16,1,16,1,8192]{4,2,3,1,0:T(8,128)(2,1)S(1)}, bf16[16,1,16,1,8192]{4,2,3,1,0:T(8,128)(2,1)}, u32[]{:S(2)}) %copy-start) | copy-done | bytes 4194328
  8.6 1.5 %collective-permute-done.1 = bf16[3,64,128]{2,1,0:T(8,128)(2,1)S(1)} collective-permute-done((bf16[3,64,128]{2,1,0:T(8,128)(2,1)S(1)}, bf16[3,64,128]{2,1,0:T(8,128)(2,1)S(1)}, u32[]{:S(2)}, u32[]{:S(2)}) %collective-permute-start.1) | collective-permute-done | bytes 49184 | tf_op jit(solution)/shard_map/ppermute | solution.py:550
  10.1 2.2 %collective-permute-start.5 = (bf16[4,1,64,128]{3,2,1,0:T(8,128)(2,1)S(1)}, bf16[4,1,64,128]{3,2,1,0:T(8,128)(2,1)S(1)}, u32[]{:S(2)}, u32[]{:S(2)}) collective-permute-start(bf16[4,1,64,128]{3,2,1,0:T(8,128)(2,1)S(1)} %get-tuple-element.65), channel_id=1, source_target_pairs={{0,24},{4,28},{8,16},{12,20},{16,8},{20,12},{24,0},{28,4},{1,25},{... | collective-permute-start | bytes 196616 | tf_op jit(solution)/shard_map/ppermute | solution.py:550
  12.9 1.4 %collective-permute-done.5 = bf16[4,1,64,128]{3,2,1,0:T(8,128)(2,1)S(1)} collective-permute-done((bf16[4,1,64,128]{3,2,1,0:T(8,128)(2,1)S(1)}, bf16[4,1,64,128]{3,2,1,0:T(8,128)(2,1)S(1)}, u32[]{:S(2)}, u32[]{:S(2)}) %collective-permute-start.5) | collective-permute-done | bytes 65568 | tf_op jit(solution)/shard_map/ppermute | solution.py:550
  14.2 1.3 %collective-permute-done.4 = bf16[4,1,64,128]{3,2,0,1:T(8,128)(2,1)S(1)} collective-permute-done((bf16[4,1,64,128]{3,2,0,1:T(8,128)(2,1)S(1)}, bf16[4,1,64,128]{3,2,0,1:T(8,128)(2,1)S(1)}, u32[]{:S(2)}, u32[]{:S(2)}) %collective-permute-start.4) | collective-permute-done | bytes 65568 | tf_op jit(solution)/shard_map/ppermute | solution.py:550
  15.5 0.7 collective-permute-done.3
  16.2 2.9 %collective-permute-start.9 = (bf16[4,4,1,64,128]{4,3,1,2,0:T(8,128)(2,1)S(1)}, bf16[4,4,1,64,128]{4,3,1,2,0:T(8,128)(2,1)S(1)}, u32[]{:S(2)}, u32[]{:S(2)}) collective-permute-start(bf16[4,4,1,64,128]{4,3,1,2,0:T(8,128)(2,1)S(1)} %pad_maximum_fusion.2), channel_id=1, source_target_pairs={{0,4},{4,0},{8,12},{12,8},{16,20},{20,16},{24,28},{28,24},{1,5},{5... | collective-permute-start | bytes 786440 | tf_op jit(solution)/shard_map/ppermute | solution.py:550
  19.2 1.8 %collective-permute-start.11 = (bf16[896,256]{1,0:T(8,128)(2,1)S(1)}, bf16[896,256]{1,0:T(8,128)(2,1)S(1)}, u32[]{:S(2)}, u32[]{:S(2)}) collective-permute-start(bf16[896,256]{1,0:T(8,128)(2,1)S(1)} %shard_map.18.refs_0_), channel_id=1, source_target_pairs={{0,3},{1,2},{2,1},{3,0},{4,7},{5,6},{6,5},{7,4},{8,11},{9,10},{10,... | collective-permute-start | bytes 1376264 | tf_op jit(solution)/shard_map/ppermute | solution.py:550
  21.2 1.2 %collective-permute-start.8 = (bf16[4,2,64,128]{3,2,1,0:T(8,128)(2,1)S(1)}, bf16[4,2,64,128]{3,2,1,0:T(8,128)(2,1)S(1)}, u32[]{:S(2)}, u32[]{:S(2)}) collective-permute-start(bf16[4,2,64,128]{3,2,1,0:T(8,128)(2,1)S(1)} %slice.15), channel_id=1, source_target_pairs={{0,24},{4,28},{8,16},{12,20},{16,8},{20,12},{24,0},{28,4},{1,25},{... | collective-permute-start | bytes 393224 | tf_op jit(solution)/shard_map/ppermute | solution.py:550
  22.6 1.2 %collective-permute-start.6 = (bf16[4,2,64,128]{3,2,1,0:T(8,128)(2,1)S(1)}, bf16[4,2,64,128]{3,2,1,0:T(8,128)(2,1)S(1)}, u32[]{:S(2)}, u32[]{:S(2)}) collective-permute-start(bf16[4,2,64,128]{3,2,1,0:T(8,128)(2,1)S(1)} %slice.15), channel_id=1, source_target_pairs={{0,8},{4,12},{8,0},{12,4},{16,24},{20,28},{24,16},{28,20},{1,9},{5... | collective-permute-start | bytes 393224 | tf_op jit(solution)/shard_map/ppermute | solution.py:550
  23.9 18.0 %shard_map.19 = (f32[64,128]{1,0:T(8,128)S(1)}, bf16[512,1536]{1,0:T(8,128)(2,1)S(1)}, f32[512,512]{1,0:T(8,128)S(1)}) custom-call(s32[2]{0:T(128)S(1)} %pad_add_fusion.place, bf16[4,4,1,64,128]{4,3,2,1,0:T(8,128)(2,1)S(1)} %bitcast.35, bf16[4,4,1,64,128]{4,3,2,1,0:T(8,128)(2,1)S(1)} %bitcast.37), custom_call_target="tpu_custom_call" | custom-call | flops 40000000000 | bytes 4194304 | tf_op jit(solution)/shard_map/pallas_call | solution.py:366
  41.9 1.3 %collective-permute-done.10.refs_1_ = bf16[896,256]{1,0:T(8,128)(2,1)S(1)} collective-permute-done((bf16[896,256]{1,0:T(8,128)(2,1)S(1)}, bf16[896,256]{1,0:T(8,128)(2,1)S(1)}, u32[]{:S(2)}, u32[]{:S(2)}) %collective-permute-start.10) | collective-permute-done | bytes 458784 | tf_op jit(solution)/shard_map/ppermute | solution.py:550
  43.2 0.6 collective-permute-start.15
  43.9 1.2 %collective-permute-start.14 = (bf16[128,1792]{1,0:T(8,128)(2,1)S(1)}, bf16[128,1792]{1,0:T(8,128)(2,1)S(1)}, u32[]{:S(2)}, u32[]{:S(2)}) collective-permute-start(bf16[128,1792]{1,0:T(8,128)(2,1)S(1)} %get-tuple-element.49.refs_0_), channel_id=1, source_target_pairs={{0,24},{4,28},{8,16},{12,20},{16,8},{20,12},{24,0},{28,4},{1,25},{... | collective-permute-start | bytes 1376264 | tf_op jit(solution)/shard_map/ppermute | solution.py:550
  45.3 1.2 %collective-permute-start.12 = (bf16[128,1792]{1,0:T(8,128)(2,1)S(1)}, bf16[128,1792]{1,0:T(8,128)(2,1)S(1)}, u32[]{:S(2)}, u32[]{:S(2)}) collective-permute-start(bf16[128,1792]{1,0:T(8,128)(2,1)S(1)} %get-tuple-element.49.refs_0_), channel_id=1, source_target_pairs={{0,8},{4,12},{8,0},{12,4},{16,24},{20,28},{24,16},{28,20},{1,9},{5... | collective-permute-start | bytes 1376264 | tf_op jit(solution)/shard_map/ppermute | solution.py:550
  46.6 1.1 %collective-permute-start.16 = (bf16[896,256]{1,0:T(8,128)(2,1)S(1)}, bf16[896,256]{1,0:T(8,128)(2,1)S(1)}, u32[]{:S(2)}, u32[]{:S(2)}) collective-permute-start(bf16[896,256]{1,0:T(8,128)(2,1)S(1)} %shard_map.18.refs_0_), channel_id=1, source_target_pairs={{0,2},{1,3},{2,0},{3,1},{4,6},{5,7},{6,4},{7,5},{8,10},{9,11},{10,... | collective-permute-start | bytes 1376264 | tf_op jit(solution)/shard_map/ppermute | solution.py:550
  47.6 19.6 %shard_map.20 = (f32[64,128]{1,0:T(8,128)S(1)}, bf16[512,1536]{1,0:T(8,128)(2,1)S(1)}, f32[512,512]{1,0:T(8,128)S(1)}, bf16[512,512]{1,0:T(8,128)(2,1)S(1)}, f32[64,128]{1,0:T(8,128)S(1)}) custom-call(s32[2]{0:T(128)S(1)} %pad_add_fusion.place, bf16[4,4,2,64,128]{4,3,2,1,0:T(8,128)(2,1)S(1)} %pad_maximum_fusion.1.near, ...), custom_call_target="tpu_custom_call" | custom-call | flops 40000000000 | bytes 4194304 | tf_op jit(solution)/shard_map/pallas_call | solution.py:366
  67.2 1.9 %collective-permute-done.16.refs_2_ = bf16[896,256]{1,0:T(8,128)(2,1)S(1)} collective-permute-done((bf16[896,256]{1,0:T(8,128)(2,1)S(1)}, bf16[896,256]{1,0:T(8,128)(2,1)S(1)}, u32[]{:S(2)}, u32[]{:S(2)}) %collective-permute-start.16) | collective-permute-done | bytes 458784 | tf_op jit(solution)/shard_map/ppermute | solution.py:550
  69.4 1.2 %collective-permute-start.17 = (bf16[4,128,1792]{2,1,0:T(8,128)(2,1)S(1)}, bf16[4,128,1792]{2,1,0:T(8,128)(2,1)S(1)}, u32[]{:S(2)}, u32[]{:S(2)}) collective-permute-start(bf16[4,128,1792]{2,1,0:T(8,128)(2,1)S(1)} %pad_maximum_fusion), channel_id=1, source_target_pairs={{0,4},{4,0},{8,12},{12,8},{16,20},{20,16},{24,28},{28,24},{1,5},{5... | collective-permute-start | bytes 5505032 | tf_op jit(solution)/shard_map/ppermute | solution.py:550
  70.5 5.9 %shard_map.21 = (bf16[896,1024]{1,0:T(8,128)(2,1)S(1)}, f32[896,256]{1,0:T(8,128)S(1)}) custom-call(s32[2]{0:T(128)S(1)} %pad_add_fusion.place, bf16[896,256]{1,0:T(8,128)(2,1)S(1)} %shard_map.18.refs_0_, bf16[896,256]{1,0:T(8,128)(2,1)S(1)} %collective-permute-done.10.refs_1_, bf16[896,256]{1,0:T(8,128)(2,1)S(1)} %collective-permute-done.16.refs_2_, ...), custom_call_target="tpu_custom_call" | custom-call | flops 2818572288 | bytes 10485760 | tf_op jit(solution)/shard_map/pallas_call | solution.py:423
  76.4 17.6 %shard_map.22 = f32[16,16,64,128]{3,2,1,0:T(8,128)} custom-call(s32[2]{0:T(128)S(1)} %pad_add_fusion.place, bf16[16,16,8192]{2,1,0:T(8,128)(2,1)} %bitcast.29, bf16[128,1792]{1,0:T(8,128)(2,1)S(1)} %get-tuple-element.49.refs_0_, bf16[128,1792]{1,0:T(8,128)(2,1)S(1)} %collective-permute-done.12.refs_1_, ...), custom_call_target="tpu_custom_call" | custom-call | flops 10000000000 | bytes 25165824 | tf_op jit(solution)/shard_map/pallas_call | solution.py:529
  (28 shorter events, 2.4 us)
Async XLA Ops:
  1.5 7.1 %collective-permute-start.2 = (bf16[3,64,128]{2,1,0:T(8,128)(2,1)S(1)}, bf16[3,64,128]{2,1,0:T(8,128)(2,1)S(1)}, u32[]{:S(2)}, u32[]{:S(2)}) collective-permute-start(bf16[3,64,128]{2,1,0:T(8,128)(2,1)S(1)} %get-tuple-element.34), channel_id=1, source_target_pairs={{0,3},{1,2},{2,1},{3,0},{4,7},{5,6},{6,5},{7,4},{8,11},{9,10},{10,... | collective-permute-start | bytes 147464 | tf_op jit(solution)/shard_map/ppermute | solution.py:550
  5.7 4.4 %collective-permute-start.1 = (bf16[3,64,128]{2,1,0:T(8,128)(2,1)S(1)}, bf16[3,64,128]{2,1,0:T(8,128)(2,1)S(1)}, u32[]{:S(2)}, u32[]{:S(2)}) collective-permute-start(bf16[3,64,128]{2,1,0:T(8,128)(2,1)S(1)} %get-tuple-element.34), channel_id=1, source_target_pairs={{0,2},{1,3},{2,0},{3,1},{4,6},{5,7},{6,4},{7,5},{8,10},{9,11},{10,... | collective-permute-start | bytes 147464 | tf_op jit(solution)/shard_map/ppermute | solution.py:550
  5.7 4.4 %collective-permute-start = (bf16[3,64,128]{2,1,0:T(8,128)(2,1)S(1)}, bf16[3,64,128]{2,1,0:T(8,128)(2,1)S(1)}, u32[]{:S(2)}, u32[]{:S(2)}) collective-permute-start(bf16[3,64,128]{2,1,0:T(8,128)(2,1)S(1)} %get-tuple-element.34), channel_id=1, source_target_pairs={{0,1},{1,0},{2,3},{3,2},{4,5},{5,4},{6,7},{7,6},{8,9},{9,8},{10,11... | collective-permute-start | bytes 147464 | tf_op jit(solution)/shard_map/ppermute | solution.py:550
  6.1 2.2 %copy-start = (bf16[16,1,16,1,8192]{4,2,3,1,0:T(8,128)(2,1)S(1)}, bf16[16,1,16,1,8192]{4,2,3,1,0:T(8,128)(2,1)}, u32[]{:S(2)}) copy-start(bf16[16,1,16,1,8192]{4,2,3,1,0:T(8,128)(2,1)} %param.1) | copy-start | bytes 12582916
  10.1 4.1 %collective-permute-start.5 = (bf16[4,1,64,128]{3,2,1,0:T(8,128)(2,1)S(1)}, bf16[4,1,64,128]{3,2,1,0:T(8,128)(2,1)S(1)}, u32[]{:S(2)}, u32[]{:S(2)}) collective-permute-start(bf16[4,1,64,128]{3,2,1,0:T(8,128)(2,1)S(1)} %get-tuple-element.65), channel_id=1, source_target_pairs={{0,24},{4,28},{8,16},{12,20},{16,8},{20,12},{24,0},{28,4},{1,25},{... | collective-permute-start | bytes 196616 | tf_op jit(solution)/shard_map/ppermute | solution.py:550
  12.4 3.1 %collective-permute-start.4 = (bf16[4,1,64,128]{3,2,0,1:T(8,128)(2,1)S(1)}, bf16[4,1,64,128]{3,2,0,1:T(8,128)(2,1)S(1)}, u32[]{:S(2)}, u32[]{:S(2)}) collective-permute-start(bf16[4,1,64,128]{3,2,0,1:T(8,128)(2,1)S(1)} %get-tuple-element.64), channel_id=1, source_target_pairs={{0,16},{4,20},{8,24},{12,28},{16,0},{20,4},{24,8},{28,12},{1,17},{... | collective-permute-start | bytes 196616 | tf_op jit(solution)/shard_map/ppermute | solution.py:550
  12.6 3.6 %collective-permute-start.3 = (bf16[4,1,64,128]{3,2,0,1:T(8,128)(2,1)S(1)}, bf16[4,1,64,128]{3,2,0,1:T(8,128)(2,1)S(1)}, u32[]{:S(2)}, u32[]{:S(2)}) collective-permute-start(bf16[4,1,64,128]{3,2,0,1:T(8,128)(2,1)S(1)} %get-tuple-element.64), channel_id=1, source_target_pairs={{0,8},{4,12},{8,0},{12,4},{16,24},{20,28},{24,16},{28,20},{1,9},{5... | collective-permute-start | bytes 196616 | tf_op jit(solution)/shard_map/ppermute | solution.py:550
  16.2 6.4 %collective-permute-start.9 = (bf16[4,4,1,64,128]{4,3,1,2,0:T(8,128)(2,1)S(1)}, bf16[4,4,1,64,128]{4,3,1,2,0:T(8,128)(2,1)S(1)}, u32[]{:S(2)}, u32[]{:S(2)}) collective-permute-start(bf16[4,4,1,64,128]{4,3,1,2,0:T(8,128)(2,1)S(1)} %pad_maximum_fusion.2), channel_id=1, source_target_pairs={{0,4},{4,0},{8,12},{12,8},{16,20},{20,16},{24,28},{28,24},{1,5},{5... | collective-permute-start | bytes 786440 | tf_op jit(solution)/shard_map/ppermute | solution.py:550
  19.2 22.7 %collective-permute-start.11 = (bf16[896,256]{1,0:T(8,128)(2,1)S(1)}, bf16[896,256]{1,0:T(8,128)(2,1)S(1)}, u32[]{:S(2)}, u32[]{:S(2)}) collective-permute-start(bf16[896,256]{1,0:T(8,128)(2,1)S(1)} %shard_map.18.refs_0_), channel_id=1, source_target_pairs={{0,3},{1,2},{2,1},{3,0},{4,7},{5,6},{6,5},{7,4},{8,11},{9,10},{10,... | collective-permute-start | bytes 1376264 | tf_op jit(solution)/shard_map/ppermute | solution.py:550
  21.0 22.2 %collective-permute-start.10 = (bf16[896,256]{1,0:T(8,128)(2,1)S(1)}, bf16[896,256]{1,0:T(8,128)(2,1)S(1)}, u32[]{:S(2)}, u32[]{:S(2)}) collective-permute-start(bf16[896,256]{1,0:T(8,128)(2,1)S(1)} %shard_map.18.refs_0_), channel_id=1, source_target_pairs={{0,1},{1,0},{2,3},{3,2},{4,5},{5,4},{6,7},{7,6},{8,9},{9,8},{10,11... | collective-permute-start | bytes 1376264 | tf_op jit(solution)/shard_map/ppermute | solution.py:550
  21.2 20.6 %collective-permute-start.8 = (bf16[4,2,64,128]{3,2,1,0:T(8,128)(2,1)S(1)}, bf16[4,2,64,128]{3,2,1,0:T(8,128)(2,1)S(1)}, u32[]{:S(2)}, u32[]{:S(2)}) collective-permute-start(bf16[4,2,64,128]{3,2,1,0:T(8,128)(2,1)S(1)} %slice.15), channel_id=1, source_target_pairs={{0,24},{4,28},{8,16},{12,20},{16,8},{20,12},{24,0},{28,4},{1,25},{... | collective-permute-start | bytes 393224 | tf_op jit(solution)/shard_map/ppermute | solution.py:550
  22.4 19.4 %collective-permute-start.7 = (bf16[4,2,64,128]{3,2,1,0:T(8,128)(2,1)S(1)}, bf16[4,2,64,128]{3,2,1,0:T(8,128)(2,1)S(1)}, u32[]{:S(2)}, u32[]{:S(2)}) collective-permute-start(bf16[4,2,64,128]{3,2,1,0:T(8,128)(2,1)S(1)} %slice.15), channel_id=1, source_target_pairs={{0,16},{4,20},{8,24},{12,28},{16,0},{20,4},{24,8},{28,12},{1,17},{... | collective-permute-start | bytes 393224 | tf_op jit(solution)/shard_map/ppermute | solution.py:550
  22.6 19.2 %collective-permute-start.6 = (bf16[4,2,64,128]{3,2,1,0:T(8,128)(2,1)S(1)}, bf16[4,2,64,128]{3,2,1,0:T(8,128)(2,1)S(1)}, u32[]{:S(2)}, u32[]{:S(2)}) collective-permute-start(bf16[4,2,64,128]{3,2,1,0:T(8,128)(2,1)S(1)} %slice.15), channel_id=1, source_target_pairs={{0,8},{4,12},{8,0},{12,4},{16,24},{20,28},{24,16},{28,20},{1,9},{5... | collective-permute-start | bytes 393224 | tf_op jit(solution)/shard_map/ppermute | solution.py:550
  43.2 4.4 %collective-permute-start.15 = (bf16[4,4,2,64,128]{4,3,2,1,0:T(8,128)(2,1)S(1)}, bf16[4,4,2,64,128]{4,3,2,1,0:T(8,128)(2,1)S(1)}, u32[]{:S(2)}, u32[]{:S(2)}) collective-permute-start(bf16[4,4,2,64,128]{4,3,2,1,0:T(8,128)(2,1)S(1)} %pad_maximum_fusion.1.near), channel_id=1, source_target_pairs={{0,4},{4,0},{8,12},{12,8},{16,20},{20,16},{24,28},{28,24},{1,5},{5... | collective-permute-start | bytes 1572872 | tf_op jit(solution)/shard_map/ppermute | solution.py:550
  43.9 25.2 %collective-permute-start.14 = (bf16[128,1792]{1,0:T(8,128)(2,1)S(1)}, bf16[128,1792]{1,0:T(8,128)(2,1)S(1)}, u32[]{:S(2)}, u32[]{:S(2)}) collective-permute-start(bf16[128,1792]{1,0:T(8,128)(2,1)S(1)} %get-tuple-element.49.refs_0_), channel_id=1, source_target_pairs={{0,24},{4,28},{8,16},{12,20},{16,8},{20,12},{24,0},{28,4},{1,25},{... | collective-permute-start | bytes 1376264 | tf_op jit(solution)/shard_map/ppermute | solution.py:550
  45.1 24.0 %collective-permute-start.13 = (bf16[128,1792]{1,0:T(8,128)(2,1)S(1)}, bf16[128,1792]{1,0:T(8,128)(2,1)S(1)}, u32[]{:S(2)}, u32[]{:S(2)}) collective-permute-start(bf16[128,1792]{1,0:T(8,128)(2,1)S(1)} %get-tuple-element.49.refs_0_), channel_id=1, source_target_pairs={{0,16},{4,20},{8,24},{12,28},{16,0},{20,4},{24,8},{28,12},{1,17},{... | collective-permute-start | bytes 1376264 | tf_op jit(solution)/shard_map/ppermute | solution.py:550
  45.3 23.8 %collective-permute-start.12 = (bf16[128,1792]{1,0:T(8,128)(2,1)S(1)}, bf16[128,1792]{1,0:T(8,128)(2,1)S(1)}, u32[]{:S(2)}, u32[]{:S(2)}) collective-permute-start(bf16[128,1792]{1,0:T(8,128)(2,1)S(1)} %get-tuple-element.49.refs_0_), channel_id=1, source_target_pairs={{0,8},{4,12},{8,0},{12,4},{16,24},{20,28},{24,16},{28,20},{1,9},{5... | collective-permute-start | bytes 1376264 | tf_op jit(solution)/shard_map/ppermute | solution.py:550
  46.6 22.6 %collective-permute-start.16 = (bf16[896,256]{1,0:T(8,128)(2,1)S(1)}, bf16[896,256]{1,0:T(8,128)(2,1)S(1)}, u32[]{:S(2)}, u32[]{:S(2)}) collective-permute-start(bf16[896,256]{1,0:T(8,128)(2,1)S(1)} %shard_map.18.refs_0_), channel_id=1, source_target_pairs={{0,2},{1,3},{2,0},{3,1},{4,6},{5,7},{6,4},{7,5},{8,10},{9,11},{10,... | collective-permute-start | bytes 1376264 | tf_op jit(solution)/shard_map/ppermute | solution.py:550
  69.4 7.1 %collective-permute-start.17 = (bf16[4,128,1792]{2,1,0:T(8,128)(2,1)S(1)}, bf16[4,128,1792]{2,1,0:T(8,128)(2,1)S(1)}, u32[]{:S(2)}, u32[]{:S(2)}) collective-permute-start(bf16[4,128,1792]{2,1,0:T(8,128)(2,1)S(1)} %pad_maximum_fusion), channel_id=1, source_target_pairs={{0,4},{4,0},{8,12},{12,8},{16,20},{20,16},{24,28},{28,24},{1,5},{5... | collective-permute-start | bytes 5505032 | tf_op jit(solution)/shard_map/ppermute | solution.py:550

commit v2 on v1

--- a/solution.py
+++ b/solution.py
@@ -108,6 +108,13 @@
     factor_rest(rest, factor, inverse, work, done)
 
 
+def parts_dot(left_side, right_side):
+    high, middle, low = split_three(left_side)
+    left_parts = beside([high, high, high, middle, middle, low])
+    high, middle, low = split_three(right_side)
+    return fast_dot(left_parts, jnp.concatenate([high, middle, low, high, middle, high]))
+
+
 def factor_rest(rest, factor, inverse, work, done):
     order = rest.shape[0]
     inverse[...] = jnp.zeros_like(inverse)
@@ -129,16 +136,16 @@
         here = slice(start, start + BLOCK)
         block_inverse = done[:, BLOCK:]
         if start:
-            inverse[here, 0:start] = exact_dot(block_inverse, inverse[here, 0:start])
+            inverse[here, 0:start] = parts_dot(block_inverse, inverse[here, 0:start])
         inverse[here, here] = block_inverse
         if start + BLOCK < order:
             after = slice(start + BLOCK, order)
-            upper = exact_dot(block_inverse, rest[here, after])
+            upper = parts_dot(block_inverse, rest[here, after])
             lower = upper.T
             factor[after, here] = lower
-            rest[after, after] = rest[after, after] - exact_dot(lower, upper)
+            rest[after, after] = rest[after, after] - parts_dot(lower, upper)
             so_far = slice(0, start + BLOCK)
-            inverse[after, so_far] = inverse[after, so_far] - exact_dot(
+            inverse[after, so_far] = inverse[after, so_far] - parts_dot(
                 lower, inverse[here, so_far]
             )
 

time: 94.4 us -> 94.3 us (level)
  waiting for transfers between devices: 8 us -> 10.6 us
  Pallas kernels: 61.8 us -> 60.3 us
  starting transfers between devices: 20.4 us -> 19.1 us
    ppermute x18, waiting for transfers between devices: 8 us -> 10.6 us  [swap(): return lax.ppermute(value, axis, [(i, i ^ offset) for i in range(count)])]
    pallas_call x2, Pallas kernels: 37.5 us -> 36.1 us  [factor_call(): pl.pallas_call(body, in_specs=[pl.BlockSpec(memory_space=pltpu.SMEM)] + [...]
    ppermute x18, starting transfers between devices: 20.4 us -> 19.1 us  [swap(): return lax.ppermute(value, axis, [(i, i ^ offset) for i in range(count)])]
  transfers between devices with their start and end apart: 18 -> 18, of which waited for: 6 -> 6; matrix products, arithmetic and copies ran while one was open for 0% -> 0% of each run, Pallas kernels for 46% -> 45%
where the time goes in v2:
time: 94.3 us; the launch traced here: 94 us
  Pallas kernels  60.3 us (64%)
  starting transfers between devices  19.1 us (20%)
  waiting for transfers between devices  10.6 us (11%)
  local copies, waits for them, and re-layouts  3.3 us (3%)
    pallas_call x2, Pallas kernels, factor_call(): pl.pallas_call(body, in_specs=[pl.BlockSpec(memory_space=pltpu.SMEM)] + [...  36.1 us
    ppermute x18, starting transfers between devices, swap(): return lax.ppermute(value, axis, [(i, i ^ offset) for i in range(count)])  19.1 us
    pallas_call x1, Pallas kernels, solve_cols(): pl.pallas_call(functools.partial(cols_kernel, chips), in_specs=[pl.BlockS...  17.6 us
    ppermute x18, waiting for transfers between devices, swap(): return lax.ppermute(value, axis, [(i, i ^ offset) for i in range(count)])  10.6 us
    pallas_call x1, Pallas kernels, solve_rows(): pl.pallas_call(rows_kernel, grid=(1,), in_specs=[pl.BlockSpec(memory_spac...  5.88 us
    unnamed x2, local copies, waits for them, and re-layouts  2.19 us
  transfers between devices with their start and end apart: 18, of which 6 were waited for; matrix products, arithmetic and copies ran while one was open for 0% of the time, Pallas kernels for 45%

profile of v2, /device:TPU:1, one launch (start us, length us, event | category | flops | bytes accessed | tf_op | source)
XLA Modules:
  0.0 94.0 jit_solution(9605073089716782848)
XLA Ops:
  0.0 1.1 %slice_bitcast_fusion.tiles = bf16[2,16,8192]{2,1,0:T(8,128)(2,1)S(1)} fusion(bf16[16,1,16,1,8192]{4,2,0,3,1:T(8,128)(2,1)} %bitcast.28), kind=kLoop, calls=%fused_computation.1 | loop fusion | bytes 1048576 | tf_op jit(solution)/shard_map/slice | solution.py:568
  1.1 0.4 shard_map.17
  1.5 4.2 %collective-permute-start.2 = (bf16[3,64,128]{2,1,0:T(8,128)(2,1)S(1)}, bf16[3,64,128]{2,1,0:T(8,128)(2,1)S(1)}, u32[]{:S(2)}, u32[]{:S(2)}) collective-permute-start(bf16[3,64,128]{2,1,0:T(8,128)(2,1)S(1)} %get-tuple-element.34), channel_id=1, source_target_pairs={{0,3},{1,2},{2,1},{3,0},{4,7},{5,6},{6,5},{7,4},{8,11},{9,10},{10,... | collective-permute-start | bytes 147464 | tf_op jit(solution)/shard_map/ppermute | solution.py:557
  6.1 2.2 %copy-done = bf16[16,1,16,1,8192]{4,2,3,1,0:T(8,128)(2,1)S(1)} copy-done((bf16[16,1,16,1,8192]{4,2,3,1,0:T(8,128)(2,1)S(1)}, bf16[16,1,16,1,8192]{4,2,3,1,0:T(8,128)(2,1)}, u32[]{:S(2)}) %copy-start) | copy-done | bytes 4194328
  8.6 1.5 %collective-permute-done.1 = bf16[3,64,128]{2,1,0:T(8,128)(2,1)S(1)} collective-permute-done((bf16[3,64,128]{2,1,0:T(8,128)(2,1)S(1)}, bf16[3,64,128]{2,1,0:T(8,128)(2,1)S(1)}, u32[]{:S(2)}, u32[]{:S(2)}) %collective-permute-start.1) | collective-permute-done | bytes 49184 | tf_op jit(solution)/shard_map/ppermute | solution.py:557
  10.1 2.2 %collective-permute-start.5 = (bf16[4,1,64,128]{3,2,1,0:T(8,128)(2,1)S(1)}, bf16[4,1,64,128]{3,2,1,0:T(8,128)(2,1)S(1)}, u32[]{:S(2)}, u32[]{:S(2)}) collective-permute-start(bf16[4,1,64,128]{3,2,1,0:T(8,128)(2,1)S(1)} %get-tuple-element.65), channel_id=1, source_target_pairs={{0,24},{4,28},{8,16},{12,20},{16,8},{20,12},{24,0},{28,4},{1,25},{... | collective-permute-start | bytes 196616 | tf_op jit(solution)/shard_map/ppermute | solution.py:557
  12.9 1.4 %collective-permute-done.5 = bf16[4,1,64,128]{3,2,1,0:T(8,128)(2,1)S(1)} collective-permute-done((bf16[4,1,64,128]{3,2,1,0:T(8,128)(2,1)S(1)}, bf16[4,1,64,128]{3,2,1,0:T(8,128)(2,1)S(1)}, u32[]{:S(2)}, u32[]{:S(2)}) %collective-permute-start.5) | collective-permute-done | bytes 65568 | tf_op jit(solution)/shard_map/ppermute | solution.py:557
  14.2 1.3 %collective-permute-done.4 = bf16[4,1,64,128]{3,2,0,1:T(8,128)(2,1)S(1)} collective-permute-done((bf16[4,1,64,128]{3,2,0,1:T(8,128)(2,1)S(1)}, bf16[4,1,64,128]{3,2,0,1:T(8,128)(2,1)S(1)}, u32[]{:S(2)}, u32[]{:S(2)}) %collective-permute-start.4) | collective-permute-done | bytes 65568 | tf_op jit(solution)/shard_map/ppermute | solution.py:557
  15.5 0.7 collective-permute-done.3
  16.2 2.9 %collective-permute-start.9 = (bf16[4,4,1,64,128]{4,3,1,2,0:T(8,128)(2,1)S(1)}, bf16[4,4,1,64,128]{4,3,1,2,0:T(8,128)(2,1)S(1)}, u32[]{:S(2)}, u32[]{:S(2)}) collective-permute-start(bf16[4,4,1,64,128]{4,3,1,2,0:T(8,128)(2,1)S(1)} %pad_maximum_fusion.2), channel_id=1, source_target_pairs={{0,4},{4,0},{8,12},{12,8},{16,20},{20,16},{24,28},{28,24},{1,5},{5... | collective-permute-start | bytes 786440 | tf_op jit(solution)/shard_map/ppermute | solution.py:557
  19.2 1.8 %collective-permute-start.11 = (bf16[896,256]{1,0:T(8,128)(2,1)S(1)}, bf16[896,256]{1,0:T(8,128)(2,1)S(1)}, u32[]{:S(2)}, u32[]{:S(2)}) collective-permute-start(bf16[896,256]{1,0:T(8,128)(2,1)S(1)} %shard_map.18.refs_0_), channel_id=1, source_target_pairs={{0,3},{1,2},{2,1},{3,0},{4,7},{5,6},{6,5},{7,4},{8,11},{9,10},{10,... | collective-permute-start | bytes 1376264 | tf_op jit(solution)/shard_map/ppermute | solution.py:557
  21.2 1.2 %collective-permute-start.8 = (bf16[4,2,64,128]{3,2,1,0:T(8,128)(2,1)S(1)}, bf16[4,2,64,128]{3,2,1,0:T(8,128)(2,1)S(1)}, u32[]{:S(2)}, u32[]{:S(2)}) collective-permute-start(bf16[4,2,64,128]{3,2,1,0:T(8,128)(2,1)S(1)} %slice.15), channel_id=1, source_target_pairs={{0,24},{4,28},{8,16},{12,20},{16,8},{20,12},{24,0},{28,4},{1,25},{... | collective-permute-start | bytes 393224 | tf_op jit(solution)/shard_map/ppermute | solution.py:557
  22.6 1.2 %collective-permute-start.6 = (bf16[4,2,64,128]{3,2,1,0:T(8,128)(2,1)S(1)}, bf16[4,2,64,128]{3,2,1,0:T(8,128)(2,1)S(1)}, u32[]{:S(2)}, u32[]{:S(2)}) collective-permute-start(bf16[4,2,64,128]{3,2,1,0:T(8,128)(2,1)S(1)} %slice.15), channel_id=1, source_target_pairs={{0,8},{4,12},{8,0},{12,4},{16,24},{20,28},{24,16},{28,20},{1,9},{5... | collective-permute-start | bytes 393224 | tf_op jit(solution)/shard_map/ppermute | solution.py:557
  23.9 17.3 %shard_map.19 = (f32[64,128]{1,0:T(8,128)S(1)}, bf16[512,1536]{1,0:T(8,128)(2,1)S(1)}, f32[512,512]{1,0:T(8,128)S(1)}) custom-call(s32[2]{0:T(128)S(1)} %pad_add_fusion.place, bf16[4,4,1,64,128]{4,3,2,1,0:T(8,128)(2,1)S(1)} %bitcast.35, bf16[4,4,1,64,128]{4,3,2,1,0:T(8,128)(2,1)S(1)} %bitcast.37), custom_call_target="tpu_custom_call" | custom-call | flops 40000000000 | bytes 4194304 | tf_op jit(solution)/shard_map/pallas_call | solution.py:373
  41.2 2.0 %collective-permute-done.10.refs_1_ = bf16[896,256]{1,0:T(8,128)(2,1)S(1)} collective-permute-done((bf16[896,256]{1,0:T(8,128)(2,1)S(1)}, bf16[896,256]{1,0:T(8,128)(2,1)S(1)}, u32[]{:S(2)}, u32[]{:S(2)}) %collective-permute-start.10) | collective-permute-done | bytes 458784 | tf_op jit(solution)/shard_map/ppermute | solution.py:557
  43.2 0.6 collective-permute-start.15
  43.9 1.2 %collective-permute-start.14 = (bf16[128,1792]{1,0:T(8,128)(2,1)S(1)}, bf16[128,1792]{1,0:T(8,128)(2,1)S(1)}, u32[]{:S(2)}, u32[]{:S(2)}) collective-permute-start(bf16[128,1792]{1,0:T(8,128)(2,1)S(1)} %get-tuple-element.49.refs_0_), channel_id=1, source_target_pairs={{0,24},{4,28},{8,16},{12,20},{16,8},{20,12},{24,0},{28,4},{1,25},{... | collective-permute-start | bytes 1376264 | tf_op jit(solution)/shard_map/ppermute | solution.py:557
  45.3 1.2 %collective-permute-start.12 = (bf16[128,1792]{1,0:T(8,128)(2,1)S(1)}, bf16[128,1792]{1,0:T(8,128)(2,1)S(1)}, u32[]{:S(2)}, u32[]{:S(2)}) collective-permute-start(bf16[128,1792]{1,0:T(8,128)(2,1)S(1)} %get-tuple-element.49.refs_0_), channel_id=1, source_target_pairs={{0,8},{4,12},{8,0},{12,4},{16,24},{20,28},{24,16},{28,20},{1,9},{5... | collective-permute-start | bytes 1376264 | tf_op jit(solution)/shard_map/ppermute | solution.py:557
  46.6 0.4 collective-permute-start.16
  46.9 18.8 %shard_map.20 = (f32[64,128]{1,0:T(8,128)S(1)}, bf16[512,1536]{1,0:T(8,128)(2,1)S(1)}, f32[512,512]{1,0:T(8,128)S(1)}, bf16[512,512]{1,0:T(8,128)(2,1)S(1)}, f32[64,128]{1,0:T(8,128)S(1)}) custom-call(s32[2]{0:T(128)S(1)} %pad_add_fusion.place, bf16[4,4,2,64,128]{4,3,2,1,0:T(8,128)(2,1)S(1)} %pad_maximum_fusion.1.near, ...), custom_call_target="tpu_custom_call" | custom-call | flops 40000000000 | bytes 4194304 | tf_op jit(solution)/shard_map/pallas_call | solution.py:373
  65.7 3.8 %collective-permute-done.16.refs_2_ = bf16[896,256]{1,0:T(8,128)(2,1)S(1)} collective-permute-done((bf16[896,256]{1,0:T(8,128)(2,1)S(1)}, bf16[896,256]{1,0:T(8,128)(2,1)S(1)}, u32[]{:S(2)}, u32[]{:S(2)}) %collective-permute-start.16) | collective-permute-done | bytes 458784 | tf_op jit(solution)/shard_map/ppermute | solution.py:557
  69.8 0.6 collective-permute-start.17
  70.4 5.9 %shard_map.21 = (bf16[896,1024]{1,0:T(8,128)(2,1)S(1)}, f32[896,256]{1,0:T(8,128)S(1)}) custom-call(s32[2]{0:T(128)S(1)} %pad_add_fusion.place, bf16[896,256]{1,0:T(8,128)(2,1)S(1)} %shard_map.18.refs_0_, bf16[896,256]{1,0:T(8,128)(2,1)S(1)} %collective-permute-done.10.refs_1_, bf16[896,256]{1,0:T(8,128)(2,1)S(1)} %collective-permute-done.16.refs_2_, ...), custom_call_target="tpu_custom_call" | custom-call | flops 2818572288 | bytes 10485760 | tf_op jit(solution)/shard_map/pallas_call | solution.py:430
  76.3 17.6 %shard_map.22 = f32[16,16,64,128]{3,2,1,0:T(8,128)} custom-call(s32[2]{0:T(128)S(1)} %pad_add_fusion.place, bf16[16,16,8192]{2,1,0:T(8,128)(2,1)} %bitcast.29, bf16[128,1792]{1,0:T(8,128)(2,1)S(1)} %get-tuple-element.49.refs_0_, bf16[128,1792]{1,0:T(8,128)(2,1)S(1)} %collective-permute-done.12.refs_1_, ...), custom_call_target="tpu_custom_call" | custom-call | flops 10000000000 | bytes 25165824 | tf_op jit(solution)/shard_map/pallas_call | solution.py:536
  (28 shorter events, 2.4 us)
Async XLA Ops:
  1.5 7.1 %collective-permute-start.2 = (bf16[3,64,128]{2,1,0:T(8,128)(2,1)S(1)}, bf16[3,64,128]{2,1,0:T(8,128)(2,1)S(1)}, u32[]{:S(2)}, u32[]{:S(2)}) collective-permute-start(bf16[3,64,128]{2,1,0:T(8,128)(2,1)S(1)} %get-tuple-element.34), channel_id=1, source_target_pairs={{0,3},{1,2},{2,1},{3,0},{4,7},{5,6},{6,5},{7,4},{8,11},{9,10},{10,... | collective-permute-start | bytes 147464 | tf_op jit(solution)/shard_map/ppermute | solution.py:557
  5.7 4.4 %collective-permute-start.1 = (bf16[3,64,128]{2,1,0:T(8,128)(2,1)S(1)}, bf16[3,64,128]{2,1,0:T(8,128)(2,1)S(1)}, u32[]{:S(2)}, u32[]{:S(2)}) collective-permute-start(bf16[3,64,128]{2,1,0:T(8,128)(2,1)S(1)} %get-tuple-element.34), channel_id=1, source_target_pairs={{0,2},{1,3},{2,0},{3,1},{4,6},{5,7},{6,4},{7,5},{8,10},{9,11},{10,... | collective-permute-start | bytes 147464 | tf_op jit(solution)/shard_map/ppermute | solution.py:557
  5.7 4.4 %collective-permute-start = (bf16[3,64,128]{2,1,0:T(8,128)(2,1)S(1)}, bf16[3,64,128]{2,1,0:T(8,128)(2,1)S(1)}, u32[]{:S(2)}, u32[]{:S(2)}) collective-permute-start(bf16[3,64,128]{2,1,0:T(8,128)(2,1)S(1)} %get-tuple-element.34), channel_id=1, source_target_pairs={{0,1},{1,0},{2,3},{3,2},{4,5},{5,4},{6,7},{7,6},{8,9},{9,8},{10,11... | collective-permute-start | bytes 147464 | tf_op jit(solution)/shard_map/ppermute | solution.py:557
  6.1 2.2 %copy-start = (bf16[16,1,16,1,8192]{4,2,3,1,0:T(8,128)(2,1)S(1)}, bf16[16,1,16,1,8192]{4,2,3,1,0:T(8,128)(2,1)}, u32[]{:S(2)}) copy-start(bf16[16,1,16,1,8192]{4,2,3,1,0:T(8,128)(2,1)} %param.1) | copy-start | bytes 12582916
  10.1 4.1 %collective-permute-start.5 = (bf16[4,1,64,128]{3,2,1,0:T(8,128)(2,1)S(1)}, bf16[4,1,64,128]{3,2,1,0:T(8,128)(2,1)S(1)}, u32[]{:S(2)}, u32[]{:S(2)}) collective-permute-start(bf16[4,1,64,128]{3,2,1,0:T(8,128)(2,1)S(1)} %get-tuple-element.65), channel_id=1, source_target_pairs={{0,24},{4,28},{8,16},{12,20},{16,8},{20,12},{24,0},{28,4},{1,25},{... | collective-permute-start | bytes 196616 | tf_op jit(solution)/shard_map/ppermute | solution.py:557
  12.4 3.1 %collective-permute-start.4 = (bf16[4,1,64,128]{3,2,0,1:T(8,128)(2,1)S(1)}, bf16[4,1,64,128]{3,2,0,1:T(8,128)(2,1)S(1)}, u32[]{:S(2)}, u32[]{:S(2)}) collective-permute-start(bf16[4,1,64,128]{3,2,0,1:T(8,128)(2,1)S(1)} %get-tuple-element.64), channel_id=1, source_target_pairs={{0,16},{4,20},{8,24},{12,28},{16,0},{20,4},{24,8},{28,12},{1,17},{... | collective-permute-start | bytes 196616 | tf_op jit(solution)/shard_map/ppermute | solution.py:557
  12.6 3.6 %collective-permute-start.3 = (bf16[4,1,64,128]{3,2,0,1:T(8,128)(2,1)S(1)}, bf16[4,1,64,128]{3,2,0,1:T(8,128)(2,1)S(1)}, u32[]{:S(2)}, u32[]{:S(2)}) collective-permute-start(bf16[4,1,64,128]{3,2,0,1:T(8,128)(2,1)S(1)} %get-tuple-element.64), channel_id=1, source_target_pairs={{0,8},{4,12},{8,0},{12,4},{16,24},{20,28},{24,16},{28,20},{1,9},{5... | collective-permute-start | bytes 196616 | tf_op jit(solution)/shard_map/ppermute | solution.py:557
  16.2 6.4 %collective-permute-start.9 = (bf16[4,4,1,64,128]{4,3,1,2,0:T(8,128)(2,1)S(1)}, bf16[4,4,1,64,128]{4,3,1,2,0:T(8,128)(2,1)S(1)}, u32[]{:S(2)}, u32[]{:S(2)}) collective-permute-start(bf16[4,4,1,64,128]{4,3,1,2,0:T(8,128)(2,1)S(1)} %pad_maximum_fusion.2), channel_id=1, source_target_pairs={{0,4},{4,0},{8,12},{12,8},{16,20},{20,16},{24,28},{28,24},{1,5},{5... | collective-permute-start | bytes 786440 | tf_op jit(solution)/shard_map/ppermute | solution.py:557
  19.2 22.0 %collective-permute-start.11 = (bf16[896,256]{1,0:T(8,128)(2,1)S(1)}, bf16[896,256]{1,0:T(8,128)(2,1)S(1)}, u32[]{:S(2)}, u32[]{:S(2)}) collective-permute-start(bf16[896,256]{1,0:T(8,128)(2,1)S(1)} %shard_map.18.refs_0_), channel_id=1, source_target_pairs={{0,3},{1,2},{2,1},{3,0},{4,7},{5,6},{6,5},{7,4},{8,11},{9,10},{10,... | collective-permute-start | bytes 1376264 | tf_op jit(solution)/shard_map/ppermute | solution.py:557
  21.0 22.2 %collective-permute-start.10 = (bf16[896,256]{1,0:T(8,128)(2,1)S(1)}, bf16[896,256]{1,0:T(8,128)(2,1)S(1)}, u32[]{:S(2)}, u32[]{:S(2)}) collective-permute-start(bf16[896,256]{1,0:T(8,128)(2,1)S(1)} %shard_map.18.refs_0_), channel_id=1, source_target_pairs={{0,1},{1,0},{2,3},{3,2},{4,5},{5,4},{6,7},{7,6},{8,9},{9,8},{10,11... | collective-permute-start | bytes 1376264 | tf_op jit(solution)/shard_map/ppermute | solution.py:557
  21.2 19.9 %collective-permute-start.8 = (bf16[4,2,64,128]{3,2,1,0:T(8,128)(2,1)S(1)}, bf16[4,2,64,128]{3,2,1,0:T(8,128)(2,1)S(1)}, u32[]{:S(2)}, u32[]{:S(2)}) collective-permute-start(bf16[4,2,64,128]{3,2,1,0:T(8,128)(2,1)S(1)} %slice.15), channel_id=1, source_target_pairs={{0,24},{4,28},{8,16},{12,20},{16,8},{20,12},{24,0},{28,4},{1,25},{... | collective-permute-start | bytes 393224 | tf_op jit(solution)/shard_map/ppermute | solution.py:557
  22.4 18.7 %collective-permute-start.7 = (bf16[4,2,64,128]{3,2,1,0:T(8,128)(2,1)S(1)}, bf16[4,2,64,128]{3,2,1,0:T(8,128)(2,1)S(1)}, u32[]{:S(2)}, u32[]{:S(2)}) collective-permute-start(bf16[4,2,64,128]{3,2,1,0:T(8,128)(2,1)S(1)} %slice.15), channel_id=1, source_target_pairs={{0,16},{4,20},{8,24},{12,28},{16,0},{20,4},{24,8},{28,12},{1,17},{... | collective-permute-start | bytes 393224 | tf_op jit(solution)/shard_map/ppermute | solution.py:557
  22.6 18.5 %collective-permute-start.6 = (bf16[4,2,64,128]{3,2,1,0:T(8,128)(2,1)S(1)}, bf16[4,2,64,128]{3,2,1,0:T(8,128)(2,1)S(1)}, u32[]{:S(2)}, u32[]{:S(2)}) collective-permute-start(bf16[4,2,64,128]{3,2,1,0:T(8,128)(2,1)S(1)} %slice.15), channel_id=1, source_target_pairs={{0,8},{4,12},{8,0},{12,4},{16,24},{20,28},{24,16},{28,20},{1,9},{5... | collective-permute-start | bytes 393224 | tf_op jit(solution)/shard_map/ppermute | solution.py:557
  43.2 3.7 %collective-permute-start.15 = (bf16[4,4,2,64,128]{4,3,2,1,0:T(8,128)(2,1)S(1)}, bf16[4,4,2,64,128]{4,3,2,1,0:T(8,128)(2,1)S(1)}, u32[]{:S(2)}, u32[]{:S(2)}) collective-permute-start(bf16[4,4,2,64,128]{4,3,2,1,0:T(8,128)(2,1)S(1)} %pad_maximum_fusion.1.near), channel_id=1, source_target_pairs={{0,4},{4,0},{8,12},{12,8},{16,20},{20,16},{24,28},{28,24},{1,5},{5... | collective-permute-start | bytes 1572872 | tf_op jit(solution)/shard_map/ppermute | solution.py:557
  43.9 25.7 %collective-permute-start.14 = (bf16[128,1792]{1,0:T(8,128)(2,1)S(1)}, bf16[128,1792]{1,0:T(8,128)(2,1)S(1)}, u32[]{:S(2)}, u32[]{:S(2)}) collective-permute-start(bf16[128,1792]{1,0:T(8,128)(2,1)S(1)} %get-tuple-element.49.refs_0_), channel_id=1, source_target_pairs={{0,24},{4,28},{8,16},{12,20},{16,8},{20,12},{24,0},{28,4},{1,25},{... | collective-permute-start | bytes 1376264 | tf_op jit(solution)/shard_map/ppermute | solution.py:557
  45.1 24.4 %collective-permute-start.13 = (bf16[128,1792]{1,0:T(8,128)(2,1)S(1)}, bf16[128,1792]{1,0:T(8,128)(2,1)S(1)}, u32[]{:S(2)}, u32[]{:S(2)}) collective-permute-start(bf16[128,1792]{1,0:T(8,128)(2,1)S(1)} %get-tuple-element.49.refs_0_), channel_id=1, source_target_pairs={{0,16},{4,20},{8,24},{12,28},{16,0},{20,4},{24,8},{28,12},{1,17},{... | collective-permute-start | bytes 1376264 | tf_op jit(solution)/shard_map/ppermute | solution.py:557
  45.3 24.2 %collective-permute-start.12 = (bf16[128,1792]{1,0:T(8,128)(2,1)S(1)}, bf16[128,1792]{1,0:T(8,128)(2,1)S(1)}, u32[]{:S(2)}, u32[]{:S(2)}) collective-permute-start(bf16[128,1792]{1,0:T(8,128)(2,1)S(1)} %get-tuple-element.49.refs_0_), channel_id=1, source_target_pairs={{0,8},{4,12},{8,0},{12,4},{16,24},{20,28},{24,16},{28,20},{1,9},{5... | collective-permute-start | bytes 1376264 | tf_op jit(solution)/shard_map/ppermute | solution.py:557
  46.6 23.0 %collective-permute-start.16 = (bf16[896,256]{1,0:T(8,128)(2,1)S(1)}, bf16[896,256]{1,0:T(8,128)(2,1)S(1)}, u32[]{:S(2)}, u32[]{:S(2)}) collective-permute-start(bf16[896,256]{1,0:T(8,128)(2,1)S(1)} %shard_map.18.refs_0_), channel_id=1, source_target_pairs={{0,2},{1,3},{2,0},{3,1},{4,6},{5,7},{6,4},{7,5},{8,10},{9,11},{10,... | collective-permute-start | bytes 1376264 | tf_op jit(solution)/shard_map/ppermute | solution.py:557
  69.8 6.5 %collective-permute-start.17 = (bf16[4,128,1792]{2,1,0:T(8,128)(2,1)S(1)}, bf16[4,128,1792]{2,1,0:T(8,128)(2,1)S(1)}, u32[]{:S(2)}, u32[]{:S(2)}) collective-permute-start(bf16[4,128,1792]{2,1,0:T(8,128)(2,1)S(1)} %pad_maximum_fusion), channel_id=1, source_target_pairs={{0,4},{4,0},{8,12},{12,8},{16,20},{20,16},{24,28},{28,24},{1,5},{5... | collective-permute-start | bytes 5505032 | tf_op jit(solution)/shard_map/ppermute | solution.py:557
